TPU v7x, 128 devices: a whole 4x4x4 slice. The times are simulated.
128 devices in a mesh: lat: 16 (over z_lo, x, core), lev: 8 (over y, z_hi).
Axes of the slice: x: 4, y: 4, z: 4 (z_hi: 2, z_lo: 2; z = z_hi * 2 + z_lo), core: 2. Of those that a mesh axis runs over, the one named last changes fastest.
Arguments:
- tracers: float32 [8, 128, 104, 1152], P(None, 'lat', 'lev'), may hold values from -6 to 6
- courant_lon: float32 [128, 104, 1152], P('lat', 'lev'), may hold values from -0.6 to 0.6
- courant_lat: float32 [128, 104, 1152], P('lat', 'lev'), may hold values from -0.6 to 0.6
- level_counts: int32 [8], replicated, may hold values from 1 to 13, 72 in all
- thick_source: float32 [128, 72, 1152], P('lat', None, 'lev'), may hold values from 0.3 to 3
- eta_weights: float32 [72], replicated, may hold values from 0.3 to 3
Outputs:
- remapped: float32 [8, 128, 72, 1152], P(None, 'lat', None, 'lev')
Inputs may be any that keep to these rules, and one draw needn't show every extreme that they name: `level_counts`: the level counts sum to 72; the index of lev that holds the most levels holds exactly 13.
All inputs are finite; a program needn't handle non-finite values.
Results may differ from a plain program's by a relative error of at most 0.0003.
Values sent between devices are 32-bit elements; how exact they have to be, the bound alone decides.
A program may use at most 128 MiB of HBM per device.

v0:
```python
import jax
import jax.numpy as jnp
from jax import lax
from jax.sharding import PartitionSpec as P


def with_halo(x, sides, width):
    for axis, dim in sides:
        size, length = (lax.axis_size(axis), x.shape[dim])
        up = [(i, (i + 1) % size) for i in range(size - 1)]
        down = [(j, i) for i, j in up]
        last = lax.slice_in_dim(x, length - width, length, axis=dim)
        first = lax.slice_in_dim(x, 0, width, axis=dim)
        before = lax.ppermute(last, axis, up)
        after = lax.ppermute(first, axis, down)
        x = jnp.concatenate([before, x, after], axis=dim)
    return x


def from_behind(x, axis, by):
    length = lax.axis_size(axis)
    pairs = [(i, i + by) for i in range(length) if 0 <= i + by < length]
    return lax.ppermute(x, axis, pairs)


def cut_along(values, begin, finish, axis):
    return lax.slice_in_dim(values, begin, finish, axis=axis)


def ppm_flux(extended, courant, axis):
    length = extended.shape[axis]
    inner = length - 6
    face = (
        7.0 * (cut_along(extended, 1, length - 2, axis) + cut_along(extended, 2, length - 1, axis))
        - (cut_along(extended, 0, length - 3, axis) + cut_along(extended, 3, length, axis))
    ) / 12.0
    left_edge = cut_along(face, 0, inner + 2, axis)
    right_edge = cut_along(face, 1, inner + 3, axis)
    centre = cut_along(extended, 2, inner + 4, axis)
    slope = right_edge - left_edge
    curve = 6.0 * centre - 3.0 * (left_edge + right_edge)
    amount = -courant
    positive = courant * (
        cut_along(right_edge, 0, inner + 1, axis)
        - 0.5
        * courant
        * (
            cut_along(slope, 0, inner + 1, axis)
            - (1.0 - 2.0 * courant / 3.0) * cut_along(curve, 0, inner + 1, axis)
        )
    )
    negative = courant * (
        cut_along(left_edge, 1, inner + 2, axis)
        + 0.5
        * amount
        * (
            cut_along(slope, 1, inner + 2, axis)
            + (1.0 - 2.0 * amount / 3.0) * cut_along(curve, 1, inner + 2, axis)
        )
    )
    return jnp.where(courant >= 0.0, positive, negative)


def periodic_flux(field, courant):
    before = jnp.roll(field, 1, axis=-1)
    before_two = jnp.roll(field, 2, axis=-1)
    after = jnp.roll(field, -1, axis=-1)
    left_edge = (7.0 * (before + field) - (before_two + after)) / 12.0
    right_edge = jnp.roll(left_edge, -1, axis=-1)
    slope = right_edge - left_edge
    curve = 6.0 * field - 3.0 * (left_edge + right_edge)
    right_west = jnp.roll(right_edge, 1, axis=-1)
    slope_west = jnp.roll(slope, 1, axis=-1)
    curve_west = jnp.roll(curve, 1, axis=-1)
    amount = -courant
    positive = courant * (
        right_west - 0.5 * courant * (slope_west - (1.0 - 2.0 * courant / 3.0) * curve_west)
    )
    negative = courant * (left_edge + 0.5 * amount * (slope + (1.0 - 2.0 * amount / 3.0) * curve))
    return jnp.where(courant >= 0.0, positive, negative)


def slot_thickness(level_counts, thick, slot_width):
    count_total = level_counts.shape[0]
    starts = jnp.cumsum(level_counts) - level_counts
    slot_ids = jnp.arange(count_total * slot_width, dtype=jnp.int32)
    owner = slot_ids // slot_width
    offset = slot_ids - owner * slot_width
    picked = owner[:, None] == jnp.arange(count_total, dtype=jnp.int32)[None, :]
    owner_start = jnp.sum(jnp.where(picked, starts[None, :], 0), axis=1)
    owner_count = jnp.sum(jnp.where(picked, level_counts[None, :], 0), axis=1)
    valid = offset < owner_count
    level_of = jnp.where(valid, owner_start + offset, 0)
    taken = jnp.take(thick, level_of, axis=1)
    return jnp.where(valid[None, :, None], taken, 0.0)


def intersection_weights(thick, eta_weights):
    tops = jnp.cumsum(thick, axis=1)
    zero_row = jnp.zeros_like(thick[:, :1])
    source = jnp.concatenate([zero_row, tops], axis=1)
    surface = tops[:, -1:]
    total = jnp.sum(eta_weights)
    fraction = jnp.cumsum(eta_weights) / total
    target = jnp.concatenate([zero_row, surface * fraction[None, :, None]], axis=1)
    target_thick = surface * (eta_weights / total)[None, :, None]
    upper = jnp.minimum(target[:, 1:, None, :], source[:, None, 1:, :])
    lower = jnp.maximum(target[:, :-1, None, :], source[:, None, :-1, :])
    return jnp.maximum(upper - lower, 0.0) / target_thick[:, :, None, :]


def shards(tracers, courant_lon, courant_lat, level_counts, thick_source, eta_weights):
    tracer_count = tracers.shape[0]
    slot_width = tracers.shape[2]
    pieces = []
    for tracer_id in range(tracer_count):
        pieces.append(with_halo(tracers[tracer_id], (("lat", 0),), 3))
    along_lat = jnp.stack(pieces, axis=0)
    northern = from_behind(courant_lat[:1], "lat", -1)
    lat_faces = jnp.concatenate([courant_lat, northern], axis=0)
    flux_lon = periodic_flux(tracers, courant_lon[None])
    flux_lat = ppm_flux(along_lat, lat_faces, 1)
    horizontal = (
        tracers
        - (jnp.roll(flux_lon, -1, axis=-1) - flux_lon)
        - (flux_lat[:, 1:] - flux_lat[:, :-1])
    )
    thick_slots = slot_thickness(level_counts, thick_source, slot_width)
    weights = intersection_weights(thick_slots, eta_weights)

    def settle_one(block):
        return jnp.sum(weights * block[:, None], axis=2)

    moved = lax.all_to_all(horizontal, "lev", split_axis=3, concat_axis=2, tiled=True)
    return lax.map(settle_one, moved)


def solution(mesh):
    return jax.shard_map(
        shards,
        mesh=mesh,
        in_specs=(
            P(None, "lat", "lev", None),
            P("lat", "lev", None),
            P("lat", "lev", None),
            P(),
            P("lat", None, "lev"),
            P(),
        ),
        out_specs=P(None, "lat", None, "lev"),
        check_vma=False,
    )
```

profile of v0, /device:TPU:7, one launch (start us, length us, event | category | flops | bytes accessed | tf_op | source)
XLA Modules:
  0.0 878.4 jit_solution(5943410753203205127)
XLA Ops:
  0.0 4.7 fusion.42
  5.5 4.0 collective-permute-start.1
  10.2 1.9 collective-permute-start.2
  12.8 5.7 collective-permute-start.3
  19.2 1.9 collective-permute-start.4
  21.8 1.9 collective-permute-start
  23.7 1.9 slice_bitcast_fusion
  25.6 1.2 fusion.40
  27.2 3.0 fusion.19
  30.2 2.9 slice.318
  33.4 4.9 multiply_subtract_fusion
  38.3 1.2 slice.320
  39.6 5.8 fusion.23
  45.6 3.0 slice.324
  48.9 5.8 collective-permute-start.5
  54.9 1.9 collective-permute-start.6
  56.8 5.8 collective-permute-start.7
  62.6 1.9 collective-permute-start.8
  64.5 5.8 collective-permute-start.9
  71.6 1.1 copy.307
  72.7 1.0 copy.308
  73.7 1.0 copy.311
  74.7 1.0 copy.312
  75.8 2.1 collective-permute-start.10
  78.0 5.8 collective-permute-start.11
  83.8 2.2 collective-permute-start.12
  86.1 5.8 collective-permute-start.13
  92.0 1.9 collective-permute-start.14
  94.2 5.8 collective-permute-start.15
  100.3 1.9 collective-permute-start.16
  103.8 5.9 collective-permute-done.16
  109.9 4.7 fusion.14
  114.6 12.1 %slice_subtract_fusion = (f32[8,10,13,1152]{3,1,2,0:T(8,128)}, f32[8,10,13,1152]{3,1,2,0:T(8,128)}) fusion(f32[8,11,13,1152]{3,1,2,0:T(8,128)} %fusion.14, f32[8,14,13,1152]{3,1,2,0:T(8,128)S(1)} %fusion.33), kind=kLoop, calls=%fused_computation.24 | loop fusion | flops 5990400 | bytes 23961600 | tf_op jit(solution)/shard_map/sub | solution.py:40
  126.7 17.4 %fusion.7 = f32[8,9,13,1152]{3,1,2,0:T(8,128)} fusion(f32[8,10,13,1152]{3,1,2,0:T(8,128)} %get-tuple-element.128, f32[8,10,13,1152]{3,1,2,0:T(8,128)} %get-tuple-element.127, f32[8,11,13,1152]{3,1,2,0:T(8,128)} %fusion.14, f32[9,13,1152]{2,0,1:T(8,128)S(1)} %copy.342, f32[9,13,1152]{2,0,1:T(8,128)S(1)} %copy.341, f32[9,13,1152]{2,0,1:T(8,128)S(1)} %copy.339, ...), kind=kLoop, calls=%fused_computation.11 | loop fusion | flops 11860992 | bytes 28708992 | tf_op jit(solution)/shard_map/jit(_where)/select_n | solution.py:61
  144.1 6.4 fusion.16
  150.5 20.6 %copy.343 = f32[8,8,13,1152]{2,1,0,3:T(8,128)} copy(f32[8,8,13,1152]{3,1,2,0:T(8,128)} %fusion.16) | data formatting | bytes 7667712 | tf_op jit(solution)/shard_map/sub | solution.py:124
  171.1 58.5 %reshape.262 = f32[8,1,119808]{2,1,0:T(1,128)} reshape(f32[1152,8,8,13]{3,2,1,0:T(8,128)} %bitcast.134) | data formatting | bytes 7667712
  229.6 19.8 %all-to-all-start = ((f32[8,1,119808]{2,1,0:T(1,128)}), f32[8,1,119808]{2,1,0:T(1,128)}, u32[]{:S(2)}, u32[]{:S(2)}) async-start(f32[8,1,119808]{2,1,0:T(1,128)} %reshape.262), calls=%async_computation | async-start | bytes 7667712 | tf_op jit(solution)/shard_map/all_to_all | solution.py:134
  250.7 2.0 gather_fusion
  253.6 1.0 pad_slice_fusion
  254.6 1.5 copy.349
  257.8 40.1 %all-to-all-done = f32[8,1,119808]{2,1,0:T(1,128)} async-done(((f32[8,1,119808]{2,1,0:T(1,128)}), f32[8,1,119808]{2,1,0:T(1,128)}, u32[]{:S(2)}, u32[]{:S(2)}) %all-to-all-start) | async-done | bytes 3833888 | tf_op jit(solution)/shard_map/all_to_all | solution.py:134
  298.4 23.5 %reduce.2 = f32[8,119808]{1,0:T(8,128)} reduce(f32[8,1,119808]{2,1,0:T(1,128)} %all-to-all-done, f32[]{:T(128)} %broadcast.254), dimensions={1}, to_apply=%all_to_all.13.reduce_sub_computation | reduce | bytes 7667716 | tf_op jit(solution)/shard_map/all_to_all | solution.py:134
  321.9 57.5 %reshape.263 = f32[1152,8,8,13]{3,2,1,0:T(8,128)} reshape(f32[8,119808]{1,0:T(8,128)} %reduce.2) | data formatting | bytes 7667712
  379.4 27.0 %copy.344 = f32[8,8,13,8,144]{4,1,2,3,0:T(8,128)} copy(f32[8,8,13,8,144]{2,1,0,4,3:T(8,128)} %bitcast.135) | data formatting | bytes 7667712 | tf_op jit(solution)/shard_map/all_to_all | solution.py:134
  406.4 6.5 copy.347
  412.9 465.0 %while.11 = (s32[]{:T(128)}, f32[8,8,72,144]{3,2,1,0:T(8,128)}, f32[8,8,104,144]{2,3,1,0:T(8,128)}, f32[8,104,144]{1,2,0:T(8,128)S(1)}, f32[8,72,144]{2,1,0:T(8,...) while((s32[]{:T(128)}, f32[8,8,72,144]{3,2,1,0:T(8,128)}, ...), condition=%wide.region_8.9_spmd.clone, body=%wide.region_6.8_spmd.clone.sunk | while | flops 60300288 | bytes 4645473 | solution.py:135
  413.2 1.1 dynamic-slice_bitcast_fusion.2
  414.3 56.1 %fusion.44 = f32[8,72,144]{2,1,0:T(8,128)S(1)} fusion(f32[8,72,144]{2,1,0:T(8,128)S(1)} %get-tuple-element.243, f32[8,104,144]{1,2,0:T(8,128)S(1)} %get-tuple-element.241, f32[8,72,144]{2,1,0:T(8,128)S(1)} %get-tuple-element.242, f32[8,104,144]{1,2,0:T(8,128)S(1)} %get-tuple-element.239, f32[8,72,144]{2,1,0:T(8,128)S(1)} %get-tuple-element.240, ...), kind=kLoop, calls=%fused_computation.3.clone.1 | loop fusion | flops 60300288 | bytes 2764800 | tf_op jit(solution)/shard_map/while/body/eval_jaxpr/reduce_sum | solution.py:132
  470.4 0.9 bitcast_dynamic-update-slice_fusion.2
  471.3 1.1 dynamic-slice_bitcast_fusion.2
  472.4 56.1 %fusion.44 = f32[8,72,144]{2,1,0:T(8,128)S(1)} fusion(f32[8,72,144]{2,1,0:T(8,128)S(1)} %get-tuple-element.243, f32[8,104,144]{1,2,0:T(8,128)S(1)} %get-tuple-element.241, f32[8,72,144]{2,1,0:T(8,128)S(1)} %get-tuple-element.242, f32[8,104,144]{1,2,0:T(8,128)S(1)} %get-tuple-element.239, f32[8,72,144]{2,1,0:T(8,128)S(1)} %get-tuple-element.240, ...), kind=kLoop, calls=%fused_computation.3.clone.1 | loop fusion | flops 60300288 | bytes 2764800 | tf_op jit(solution)/shard_map/while/body/eval_jaxpr/reduce_sum | solution.py:132
  529.4 1.1 dynamic-slice_bitcast_fusion.2
  530.5 56.1 %fusion.44 = f32[8,72,144]{2,1,0:T(8,128)S(1)} fusion(f32[8,72,144]{2,1,0:T(8,128)S(1)} %get-tuple-element.243, f32[8,104,144]{1,2,0:T(8,128)S(1)} %get-tuple-element.241, f32[8,72,144]{2,1,0:T(8,128)S(1)} %get-tuple-element.242, f32[8,104,144]{1,2,0:T(8,128)S(1)} %get-tuple-element.239, f32[8,72,144]{2,1,0:T(8,128)S(1)} %get-tuple-element.240, ...), kind=kLoop, calls=%fused_computation.3.clone.1 | loop fusion | flops 60300288 | bytes 2764800 | tf_op jit(solution)/shard_map/while/body/eval_jaxpr/reduce_sum | solution.py:132
  587.5 1.1 dynamic-slice_bitcast_fusion.2
  588.6 56.1 %fusion.44 = f32[8,72,144]{2,1,0:T(8,128)S(1)} fusion(f32[8,72,144]{2,1,0:T(8,128)S(1)} %get-tuple-element.243, f32[8,104,144]{1,2,0:T(8,128)S(1)} %get-tuple-element.241, f32[8,72,144]{2,1,0:T(8,128)S(1)} %get-tuple-element.242, f32[8,104,144]{1,2,0:T(8,128)S(1)} %get-tuple-element.239, f32[8,72,144]{2,1,0:T(8,128)S(1)} %get-tuple-element.240, ...), kind=kLoop, calls=%fused_computation.3.clone.1 | loop fusion | flops 60300288 | bytes 2764800 | tf_op jit(solution)/shard_map/while/body/eval_jaxpr/reduce_sum | solution.py:132
  645.6 1.1 dynamic-slice_bitcast_fusion.2
  646.7 56.1 %fusion.44 = f32[8,72,144]{2,1,0:T(8,128)S(1)} fusion(f32[8,72,144]{2,1,0:T(8,128)S(1)} %get-tuple-element.243, f32[8,104,144]{1,2,0:T(8,128)S(1)} %get-tuple-element.241, f32[8,72,144]{2,1,0:T(8,128)S(1)} %get-tuple-element.242, f32[8,104,144]{1,2,0:T(8,128)S(1)} %get-tuple-element.239, f32[8,72,144]{2,1,0:T(8,128)S(1)} %get-tuple-element.240, ...), kind=kLoop, calls=%fused_computation.3.clone.1 | loop fusion | flops 60300288 | bytes 2764800 | tf_op jit(solution)/shard_map/while/body/eval_jaxpr/reduce_sum | solution.py:132
  703.7 1.1 dynamic-slice_bitcast_fusion.2
  704.8 56.1 %fusion.44 = f32[8,72,144]{2,1,0:T(8,128)S(1)} fusion(f32[8,72,144]{2,1,0:T(8,128)S(1)} %get-tuple-element.243, f32[8,104,144]{1,2,0:T(8,128)S(1)} %get-tuple-element.241, f32[8,72,144]{2,1,0:T(8,128)S(1)} %get-tuple-element.242, f32[8,104,144]{1,2,0:T(8,128)S(1)} %get-tuple-element.239, f32[8,72,144]{2,1,0:T(8,128)S(1)} %get-tuple-element.240, ...), kind=kLoop, calls=%fused_computation.3.clone.1 | loop fusion | flops 60300288 | bytes 2764800 | tf_op jit(solution)/shard_map/while/body/eval_jaxpr/reduce_sum | solution.py:132
  761.8 1.1 dynamic-slice_bitcast_fusion.2
  762.9 56.1 %fusion.44 = f32[8,72,144]{2,1,0:T(8,128)S(1)} fusion(f32[8,72,144]{2,1,0:T(8,128)S(1)} %get-tuple-element.243, f32[8,104,144]{1,2,0:T(8,128)S(1)} %get-tuple-element.241, f32[8,72,144]{2,1,0:T(8,128)S(1)} %get-tuple-element.242, f32[8,104,144]{1,2,0:T(8,128)S(1)} %get-tuple-element.239, f32[8,72,144]{2,1,0:T(8,128)S(1)} %get-tuple-element.240, ...), kind=kLoop, calls=%fused_computation.3.clone.1 | loop fusion | flops 60300288 | bytes 2764800 | tf_op jit(solution)/shard_map/while/body/eval_jaxpr/reduce_sum | solution.py:132
  819.9 1.1 dynamic-slice_bitcast_fusion.2
  821.0 56.1 %fusion.44 = f32[8,72,144]{2,1,0:T(8,128)S(1)} fusion(f32[8,72,144]{2,1,0:T(8,128)S(1)} %get-tuple-element.243, f32[8,104,144]{1,2,0:T(8,128)S(1)} %get-tuple-element.241, f32[8,72,144]{2,1,0:T(8,128)S(1)} %get-tuple-element.242, f32[8,104,144]{1,2,0:T(8,128)S(1)} %get-tuple-element.239, f32[8,72,144]{2,1,0:T(8,128)S(1)} %get-tuple-element.240, ...), kind=kLoop, calls=%fused_computation.3.clone.1 | loop fusion | flops 60300288 | bytes 2764800 | tf_op jit(solution)/shard_map/while/body/eval_jaxpr/reduce_sum | solution.py:132
  (136 shorter events, 19.1 us)
Async XLA Ops:
  0.0 250.6 %copy-start = (f32[8,72,144]{2,1,0:T(8,128)S(1)}, f32[8,72,144]{2,1,0:T(8,128)}, u32[]{:S(2)}) copy-start(f32[8,72,144]{2,1,0:T(8,128)} %param.12) | copy-start | bytes 995332
  0.0 23.7 %copy-start.1 = (f32[8,8,13,1152]{3,1,2,0:T(8,128)S(1)}, f32[8,8,13,1152]{3,1,2,0:T(8,128)}, u32[]{:S(2)}) copy-start(f32[8,8,13,1152]{3,1,2,0:T(8,128)} %param.8) | copy-start | bytes 11501572
  0.0 21.2 %slice-start.1 = ((f32[8,13,1152]{2,0,1:T(8,128)}), f32[1,13,1152]{2,0,1:T(1,128)S(1)}, s32[]{:S(2)}) async-start(f32[8,13,1152]{2,0,1:T(8,128)} %param.10), calls=%async_computation.2 | async-start | bytes 119808 | tf_op jit(solution)/shard_map/slice | solution.py:119
  5.5 49.4 %collective-permute-start.1 = (f32[3,13,1152]{2,1,0:T(8,128)}, f32[3,13,1152]{2,1,0:T(8,128)}, u32[]{:S(2)}, u32[]{:S(2)}) collective-permute-start(f32[3,13,1152]{2,1,0:T(8,128)} %bitcast.125), channel_id=1, source_target_pairs={{0,8},{8,16},{16,24},{24,32},{32,40},{40,48},{48,56},{56,64},{64,7... | collective-permute-start | bytes 539144 | tf_op jit(solution)/shard_map/ppermute | solution.py:14
  10.2 46.6 %collective-permute-start.2 = (f32[3,13,1152]{2,1,0:T(8,128)}, f32[3,13,1152]{2,1,0:T(8,128)}, u32[]{:S(2)}, u32[]{:S(2)}) collective-permute-start(f32[3,13,1152]{2,1,0:T(8,128)} %bitcast.124), channel_id=1, source_target_pairs={{8,0},{16,8},{24,16},{32,24},{40,32},{48,40},{56,48},{64,56},{72,6... | collective-permute-start | bytes 539144 | tf_op jit(solution)/shard_map/ppermute | solution.py:15
  12.8 49.8 %collective-permute-start.3 = (f32[3,13,1152]{2,1,0:T(8,128)}, f32[3,13,1152]{2,1,0:T(8,128)}, u32[]{:S(2)}, u32[]{:S(2)}) collective-permute-start(f32[3,13,1152]{2,1,0:T(8,128)} %bitcast.123), channel_id=1, source_target_pairs={{0,8},{8,16},{16,24},{24,32},{32,40},{40,48},{48,56},{56,64},{64,7... | collective-permute-start | bytes 539144 | tf_op jit(solution)/shard_map/ppermute | solution.py:14
  19.2 45.3 %collective-permute-start.4 = (f32[3,13,1152]{2,1,0:T(8,128)}, f32[3,13,1152]{2,1,0:T(8,128)}, u32[]{:S(2)}, u32[]{:S(2)}) collective-permute-start(f32[3,13,1152]{2,1,0:T(8,128)} %bitcast.122), channel_id=1, source_target_pairs={{8,0},{16,8},{24,16},{32,24},{40,32},{48,40},{56,48},{64,56},{72,6... | collective-permute-start | bytes 539144 | tf_op jit(solution)/shard_map/ppermute | solution.py:15
  21.8 27.0 %collective-permute-start = (f32[1,13,1152]{2,1,0:T(8,128)}, f32[1,13,1152]{2,1,0:T(8,128)S(1)}, u32[]{:S(2)}, u32[]{:S(2)}) collective-permute-start(f32[1,13,1152]{2,1,0:T(8,128)} %copy.385), channel_id=1, source_target_pairs={{8,0},{16,8},{24,16},{32,24},{40,32},{48,40},{56,48},{64,56},{72,6... | collective-permute-start | bytes 179720 | tf_op jit(solution)/shard_map/ppermute | solution.py:23
  30.2 3.0 copy-start.5
  39.6 5.8 copy-start.15
  45.4 3.1 copy-start.2
  45.4 3.1 copy-start.14
  48.9 26.9 %collective-permute-start.5 = (f32[3,13,1152]{2,1,0:T(8,128)S(1)}, f32[3,13,1152]{2,1,0:T(8,128)S(1)}, u32[]{:S(2)}, u32[]{:S(2)}) collective-permute-start(f32[3,13,1152]{2,1,0:T(8,128)S(1)} %bitcast.150), channel_id=1, source_target_pairs={{0,8},{8,16},{16,24},{24,32},{32,40},{40,48},{48,56},{56,64},{64,7... | collective-permute-start | bytes 539144 | tf_op jit(solution)/shard_map/ppermute | solution.py:14
  54.9 23.1 %collective-permute-start.6 = (f32[3,13,1152]{2,1,0:T(8,128)S(1)}, f32[3,13,1152]{2,1,0:T(8,128)S(1)}, u32[]{:S(2)}, u32[]{:S(2)}) collective-permute-start(f32[3,13,1152]{2,1,0:T(8,128)S(1)} %bitcast.149), channel_id=1, source_target_pairs={{8,0},{16,8},{24,16},{32,24},{40,32},{48,40},{56,48},{64,56},{72,6... | collective-permute-start | bytes 539144 | tf_op jit(solution)/shard_map/ppermute | solution.py:15
  56.8 27.0 %collective-permute-start.7 = (f32[3,13,1152]{2,1,0:T(8,128)S(1)}, f32[3,13,1152]{2,1,0:T(8,128)S(1)}, u32[]{:S(2)}, u32[]{:S(2)}) collective-permute-start(f32[3,13,1152]{2,1,0:T(8,128)S(1)} %bitcast.148), channel_id=1, source_target_pairs={{0,8},{8,16},{16,24},{24,32},{32,40},{40,48},{48,56},{56,64},{64,7... | collective-permute-start | bytes 539144 | tf_op jit(solution)/shard_map/ppermute | solution.py:14
  62.6 23.5 %collective-permute-start.8 = (f32[3,13,1152]{2,1,0:T(8,128)S(1)}, f32[3,13,1152]{2,1,0:T(8,128)S(1)}, u32[]{:S(2)}, u32[]{:S(2)}) collective-permute-start(f32[3,13,1152]{2,1,0:T(8,128)S(1)} %bitcast.147), channel_id=1, source_target_pairs={{8,0},{16,8},{24,16},{32,24},{40,32},{48,40},{56,48},{64,56},{72,6... | collective-permute-start | bytes 539144 | tf_op jit(solution)/shard_map/ppermute | solution.py:15
  64.5 27.5 %collective-permute-start.9 = (f32[3,13,1152]{2,1,0:T(8,128)S(1)}, f32[3,13,1152]{2,1,0:T(8,128)S(1)}, u32[]{:S(2)}, u32[]{:S(2)}) collective-permute-start(f32[3,13,1152]{2,1,0:T(8,128)S(1)} %bitcast.146), channel_id=1, source_target_pairs={{0,8},{8,16},{16,24},{24,32},{32,40},{40,48},{48,56},{56,64},{64,7... | collective-permute-start | bytes 539144 | tf_op jit(solution)/shard_map/ppermute | solution.py:14
  70.8 23.2 %copy-start.13 = (f32[8,13,1152]{2,0,1:T(8,128)S(1)}, f32[8,13,1152]{2,0,1:T(8,128)}, u32[]{:S(2)}) copy-start(f32[8,13,1152]{2,0,1:T(8,128)} %get-tuple-element.155) | copy-start | bytes 1437700
  71.0 29.1 %copy-start.12 = (f32[8,13,1152]{2,0,1:T(8,128)S(1)}, f32[8,13,1152]{2,0,1:T(8,128)}, u32[]{:S(2)}) copy-start(f32[8,13,1152]{2,0,1:T(8,128)} %get-tuple-element.152) | copy-start | bytes 1437700
  71.5 30.9 %copy-start.11 = (f32[8,13,1152]{2,0,1:T(8,128)S(1)}, f32[8,13,1152]{2,0,1:T(8,128)}, u32[]{:S(2)}) copy-start(f32[8,13,1152]{2,0,1:T(8,128)} %get-tuple-element.156) | copy-start | bytes 1437700
  75.8 26.9 %copy-start.10 = (f32[8,13,1152]{2,0,1:T(8,128)S(1)}, f32[8,13,1152]{2,0,1:T(8,128)}, u32[]{:S(2)}) copy-start(f32[8,13,1152]{2,0,1:T(8,128)} %get-tuple-element.150) | copy-start | bytes 1437700
  75.8 18.4 %collective-permute-start.10 = (f32[3,13,1152]{2,1,0:T(8,128)S(1)}, f32[3,13,1152]{2,1,0:T(8,128)S(1)}, u32[]{:S(2)}, u32[]{:S(2)}) collective-permute-start(f32[3,13,1152]{2,1,0:T(8,128)S(1)} %bitcast.145), channel_id=1, source_target_pairs={{8,0},{16,8},{24,16},{32,24},{40,32},{48,40},{56,48},{64,56},{72,6... | collective-permute-start | bytes 539144 | tf_op jit(solution)/shard_map/ppermute | solution.py:15
  78.0 22.3 %collective-permute-start.11 = (f32[3,13,1152]{2,1,0:T(8,128)S(1)}, f32[3,13,1152]{2,1,0:T(8,128)S(1)}, u32[]{:S(2)}, u32[]{:S(2)}) collective-permute-start(f32[3,13,1152]{2,1,0:T(8,128)S(1)} %bitcast.144), channel_id=1, source_target_pairs={{0,8},{8,16},{16,24},{24,32},{32,40},{40,48},{48,56},{56,64},{64,7... | collective-permute-start | bytes 539144 | tf_op jit(solution)/shard_map/ppermute | solution.py:14
  83.8 18.7 %collective-permute-start.12 = (f32[3,13,1152]{2,1,0:T(8,128)S(1)}, f32[3,13,1152]{2,1,0:T(8,128)S(1)}, u32[]{:S(2)}, u32[]{:S(2)}) collective-permute-start(f32[3,13,1152]{2,1,0:T(8,128)S(1)} %bitcast.143), channel_id=1, source_target_pairs={{8,0},{16,8},{24,16},{32,24},{40,32},{48,40},{56,48},{64,56},{72,6... | collective-permute-start | bytes 539144 | tf_op jit(solution)/shard_map/ppermute | solution.py:15
  86.1 16.7 %collective-permute-start.13 = (f32[3,13,1152]{2,1,0:T(8,128)S(1)}, f32[3,13,1152]{2,1,0:T(8,128)S(1)}, u32[]{:S(2)}, u32[]{:S(2)}) collective-permute-start(f32[3,13,1152]{2,1,0:T(8,128)S(1)} %bitcast.142), channel_id=1, source_target_pairs={{0,8},{8,16},{16,24},{24,32},{32,40},{40,48},{48,56},{56,64},{64,7... | collective-permute-start | bytes 539144 | tf_op jit(solution)/shard_map/ppermute | solution.py:14
  92.0 11.2 %collective-permute-start.14 = (f32[3,13,1152]{2,1,0:T(8,128)S(1)}, f32[3,13,1152]{2,1,0:T(8,128)S(1)}, u32[]{:S(2)}, u32[]{:S(2)}) collective-permute-start(f32[3,13,1152]{2,1,0:T(8,128)S(1)} %bitcast.141), channel_id=1, source_target_pairs={{8,0},{16,8},{24,16},{32,24},{40,32},{48,40},{56,48},{64,56},{72,6... | collective-permute-start | bytes 539144 | tf_op jit(solution)/shard_map/ppermute | solution.py:15
  94.0 8.9 %copy-start.9 = (f32[8,13,1152]{2,0,1:T(8,128)S(1)}, f32[8,13,1152]{2,0,1:T(8,128)}, u32[]{:S(2)}) copy-start(f32[8,13,1152]{2,0,1:T(8,128)} %get-tuple-element.154) | copy-start | bytes 1437700
  94.2 9.2 %collective-permute-start.15 = (f32[3,13,1152]{2,1,0:T(8,128)S(1)}, f32[3,13,1152]{2,1,0:T(8,128)S(1)}, u32[]{:S(2)}, u32[]{:S(2)}) collective-permute-start(f32[3,13,1152]{2,1,0:T(8,128)S(1)} %bitcast.140), channel_id=1, source_target_pairs={{0,8},{8,16},{16,24},{24,32},{32,40},{40,48},{48,56},{56,64},{64,7... | collective-permute-start | bytes 539144 | tf_op jit(solution)/shard_map/ppermute | solution.py:14
  100.1 3.2 copy-start.8
  100.3 9.4 %collective-permute-start.16 = (f32[3,13,1152]{2,1,0:T(8,128)S(1)}, f32[3,13,1152]{2,1,0:T(8,128)S(1)}, u32[]{:S(2)}, u32[]{:S(2)}) collective-permute-start(f32[3,13,1152]{2,1,0:T(8,128)S(1)} %bitcast.139), channel_id=1, source_target_pairs={{8,0},{16,8},{24,16},{32,24},{40,32},{48,40},{56,48},{64,56},{72,6... | collective-permute-start | bytes 539144 | tf_op jit(solution)/shard_map/ppermute | solution.py:15
  102.3 1.2 copy-start.7
  102.7 7.1 copy-start.6
  126.7 17.4 %copy-start.3 = (f32[8,8,13,1152]{3,1,2,0:T(8,128)S(1)}, f32[8,8,13,1152]{3,1,2,0:T(8,128)}, u32[]{:S(2)}) copy-start(f32[8,8,13,1152]{3,1,2,0:T(8,128)} %copy-done.2) | copy-start | bytes 11501572
  126.7 17.4 %slice-start = ((f32[8,8,13,1152]{3,1,2,0:T(8,128)}), f32[8,8,13,1]{3,1,2,0:T(8,128)S(1)}, s32[]{:S(2)}) async-start(f32[8,8,13,1152]{3,1,2,0:T(8,128)} %copy-done.2), calls=%async_computation.1 | async-start | bytes 851968 | tf_op jit(solution)/shard_map/jit(_roll_static)/slice | solution.py:125
  126.7 17.4 %copy-start.4 = (f32[8,8,13,1151]{3,1,2,0:T(8,128)S(1)}, f32[8,8,13,1151]{3,1,2,0:T(8,128)}, u32[]{:S(2)}) copy-start(f32[8,8,13,1151]{3,1,2,0:T(8,128)} %slice.324) | copy-start | bytes 11491588
  229.6 19.8 %copy-start.16 = (f32[72]{0:T(128)S(1)}, f32[72]{0:T(128)}, u32[]{:S(2)}) copy-start(f32[72]{0:T(128)} %param.13) | copy-start | bytes 868
  229.6 20.7 %copy-start.17 = (s32[8]{0:T(128)S(1)}, s32[8]{0:T(128)}, u32[]{:S(2)}) copy-start(s32[8]{0:T(128)} %param.11) | copy-start | bytes 100
  229.6 68.2 %all-to-all-start = ((f32[8,1,119808]{2,1,0:T(1,128)}), f32[8,1,119808]{2,1,0:T(1,128)}, u32[]{:S(2)}, u32[]{:S(2)}) async-start(f32[8,1,119808]{2,1,0:T(1,128)} %reshape.262), calls=%async_computation | async-start | bytes 7667712 | tf_op jit(solution)/shard_map/all_to_all | solution.py:134
where the time goes:
time: 889 us; the launch traced here: 878 us
  other arithmetic  532 us (60%)
  local copies, waits for them, and re-layouts  217 us (24%)
  starting transfers between devices  81.7 us (9%)
  waiting for transfers between devices  46 us (5%)
    reduce_sum x8, other arithmetic, settle_one(): return jnp.sum(weights * block[:, None], axis=2)  449 us
    unnamed x59, local copies, waits for them, and re-layouts  128 us
    ppermute x8, starting transfers between devices, with_halo(): before = lax.ppermute(last, axis, up)  44.3 us
    all_to_all x1, waiting for transfers between devices, shards(): lax.all_to_all(horizontal, 'lev', split_axis=3, concat_axis=2, tiled=True)  40.1 us
    all_to_all x2, local copies, waits for them, and re-layouts, shards(): lax.all_to_all(horizontal, 'lev', split_axis=3, concat_axis=2, tiled=True)  27.6 us
    all_to_all x1, other arithmetic, shards(): lax.all_to_all(horizontal, 'lev', split_axis=3, concat_axis=2, tiled=True)  23.5 us
    sub x1, local copies, waits for them, and re-layouts, shards(): tracers - (jnp.roll(flux_lon, -1, axis=-1) - flux_lon)  20.6 us
    all_to_all x1, starting transfers between devices, shards(): lax.all_to_all(horizontal, 'lev', split_axis=3, concat_axis=2, tiled=True)  19.8 us
  transfers between devices with their start and end apart: 18, of which 2 were waited for; matrix products, arithmetic and copies ran while one was open for 5% of the time, Pallas kernels for 0%

commit v1 on v0

v1 whole, which is shorter than its diff:
```python
import functools
import jax
import jax.numpy as jnp
from jax import lax
from jax.experimental import pallas as pl
from jax.experimental.pallas import tpu as pltpu
from jax.sharding import PartitionSpec as P

MESH = pl.DeviceIdType.MESH
HI = lax.Precision.HIGHEST
F32 = jnp.float32
NT, NI, NS, NX, ND = 8, 8, 13, 1152, 8
SPAN = NX // ND
ROWS = 120


def gather8(v, idx):
    return jnp.take_along_axis(v, idx, axis=0, mode="promise_in_bounds")


def face_weights(c):
    m = jnp.abs(c)
    r = 1.0 - m
    cm = c * m
    return c * r * r * (1.0 / 12.0), cm * (3.0 - 2.0 * m), cm * r * (-1.0 / 12.0)


def latitude_part(t, xs, south, north, wlat, part):
    def column(k, _):
        lanes = pl.ds(pl.multiple_of(k * 128, 128), 128)
        for lo, hi in ((0, 8), (8, NS)):
            q = [south[t, j, lo:hi, lanes] for j in range(3)]
            q += [xs[t, j, lo:hi, lanes] for j in range(NI)]
            q += [north[t, j, lo:hi, lanes] for j in range(3)]
            a = [7.0 * (q[j + 1] + q[j + 2]) - (q[j] + q[j + 3]) for j in range(NI + 3)]
            before = None
            for f in range(NI + 1):
                w0 = wlat[0, f, lo:hi, lanes]
                up = w0 >= 0.0
                flux = (
                    w0 * a[f + 1]
                    + wlat[1, f, lo:hi, lanes] * jnp.where(up, q[f + 2], q[f + 3])
                    + wlat[2, f, lo:hi, lanes] * jnp.where(up, a[f], a[f + 2])
                )
                if f > 0:
                    part[f - 1, lo:hi, lanes] = q[f + 2] - (flux - before)
                before = flux
        return 0

    lax.fori_loop(0, NX // 128, column, 0)


def longitude_part(t, xs, wlon, part, send):
    for i in range(NI):
        for lo, hi in ((0, 8), (8, NS)):
            q = xs[t, i, lo:hi, :]
            west = jnp.roll(q, 1, axis=1)
            a = 7.0 * (west + q) - (jnp.roll(q, 2, axis=1) + jnp.roll(q, -1, axis=1))
            w0 = wlon[0, i, lo:hi, :]
            up = w0 >= 0.0
            flux = (
                w0 * a
                + wlon[1, i, lo:hi, :] * jnp.where(up, west, q)
                + wlon[2, i, lo:hi, :] * jnp.where(up, jnp.roll(a, 1, axis=1), jnp.roll(a, -1, axis=1))
            )
            h = part[i, lo:hi, :] - (jnp.roll(flux, -1, axis=1) - flux)
            n = hi - lo
            base = n * i if lo == 0 else 72 + n * i
            tail = 64 if lo == 0 else 112
            for e in range(ND):
                send[t, e, base:base + n, :] = h[:, SPAN * e:SPAN * e + 128]
                send[t, e, tail:tail + n, 16 * i:16 * i + 16] = h[:, SPAN * e + 128:SPAN * e + SPAN]


def prep(cnt_ref, thick_ref, eta_ref, sl_s, h_s, idx_s, dt_s, rt_s, fr_s, th_s):
    for i in range(8):
        th_s[i] = thick_ref[i, :, 0:128]
        th_s[8, :, 16 * i:16 * i + 16] = thick_ref[i, :, 128:144]
    rows = lax.broadcasted_iota(jnp.int32, (128, 128), 0)
    lanes = lax.broadcasted_iota(jnp.int32, (128, 128), 1)
    dd, ss = rows >> 4, rows & 15
    hi = jnp.zeros((128, 128), jnp.int32)
    lo = jnp.zeros((128, 128), jnp.int32)
    start = jnp.int32(0)
    for d in range(8):
        c = cnt_ref[d]
        hi = jnp.where(dd == d, start + jnp.minimum(ss + 1, c), hi)
        lo = jnp.where(dd == d, start + jnp.minimum(ss, c), lo)
        start = start + c
    mu = jnp.where(lanes < hi, 1.0, 0.0)[:, :72]
    ml = jnp.where(lanes < lo, 1.0, 0.0)[:, :72]
    er = eta_ref[...]
    r72 = lax.broadcasted_iota(jnp.int32, (72, 72), 0)
    l72 = lax.broadcasted_iota(jnp.int32, (72, 72), 1)
    eb = jnp.broadcast_to(er, (72, 72))
    tot = jnp.sum(eb, axis=1, keepdims=True)
    cum = jnp.sum(jnp.where(l72 <= r72, eb, 0.0), axis=1, keepdims=True)
    own = jnp.sum(jnp.where(l72 == r72, eb, 0.0), axis=1, keepdims=True)
    fr_s[0] = jnp.broadcast_to(cum / tot, (72, 128))
    fr_s[1] = jnp.broadcast_to(own / tot, (72, 128))

    def one(ct, _):
        th = th_s[ct]
        su = jnp.dot(mu, th, precision=HI, preferred_element_type=jnp.float32)
        sl = jnp.dot(ml, th, precision=HI, preferred_element_type=jnp.float32)
        sl_s[0] = sl
        sl_s[1] = su
        h_s[ct] = su - sl
        ps = jnp.broadcast_to(su[127:128, :], (8, 128))
        for tb in range(9):
            t = ps * fr_s[0, 8 * tb:8 * tb + 8, :]
            rt_s[ct, 8 * tb:8 * tb + 8, :] = 1.0 / (ps * fr_s[1, 8 * tb:8 * tb + 8, :])
            n = jnp.zeros((8, 128), jnp.int32)
            for d in range(8):
                for s in range(13):
                    row = jnp.broadcast_to(sl_s[1, 16 * d + s:16 * d + s + 1, :], (8, 128))
                    n = n + jnp.where(row <= t, 1 + (3 if s == 12 else 0), 0)
            n = jnp.minimum(n, 127)
            loc = n & 7
            vb = n >> 3
            g = jnp.zeros((8, 128), jnp.float32)
            gh = jnp.zeros((8, 128), jnp.float32)
            for v in range(16):
                hit = vb == v
                g = jnp.where(hit, gather8(sl_s[0, 8 * v:8 * v + 8, :], loc), g)
                gh = jnp.where(hit, gather8(h_s[ct, 8 * v:8 * v + 8, :], loc), gh)
            idx_s[ct, 8 * tb:8 * tb + 8, :] = n
            dt_s[ct, 8 * tb:8 * tb + 8, :] = jnp.clip(t - g, 0.0, gh)
        return 0
    lax.fori_loop(0, 9, one, 0)

def remap_tile(q_of, ct, h_s, idx_s, dt_s, rt_s, c_s, q_s, f_s, tri):
    for d in range(8):
        a, b = q_of(d)
        q_s[16 * d:16 * d + 8, :] = a
        q_s[16 * d + 8:16 * d + 16, :] = b
    q = q_s[...]
    c_s[...] = jnp.dot(tri, h_s[ct] * q, precision=HI, preferred_element_type=jnp.float32)
    f_s[0:8, :] = jnp.zeros((8, 128), jnp.float32)
    for tb in range(9):
        n = idx_s[ct, 8 * tb:8 * tb + 8, :]
        loc, vb = n & 7, n >> 3
        gc = jnp.zeros((8, 128), jnp.float32)
        gq = jnp.zeros((8, 128), jnp.float32)
        for v in range(16):
            hit = vb == v
            gc = jnp.where(hit, gather8(c_s[8 * v:8 * v + 8, :], loc), gc)
            gq = jnp.where(hit, gather8(q_s[8 * v:8 * v + 8, :], loc), gq)
        f_s[8 + 8 * tb:16 + 8 * tb, :] = gc + dt_s[ct, 8 * tb:8 * tb + 8, :] * gq
    return (f_s[8:80, :] - f_s[7:79, :]) * rt_s[ct]


def kernel(lat_axis, lev_axis, cnt_ref, x_hbm, clon_hbm, clat_hbm, thick_hbm, eta_ref, out_hbm,
           xs, south, north, clon, clat, cnorth, wlat, wlon, part, send, recv, thick, stage,
           sl_s, h_s, idx_s, dt_s, rt_s, fr_s, th_s, c_s, q_s, f_s,
           x_sem, c_sem, hsend, hrecv, ssem, rsem, lsem, osem):
    lat, lev = lax.axis_index("lat"), lax.axis_index("lev")

    loads = [pltpu.make_async_copy(x_hbm.at[t], xs.at[t], x_sem.at[t]) for t in range(NT)]
    small = [pltpu.make_async_copy(clat_hbm, clat, c_sem.at[0]), pltpu.make_async_copy(clon_hbm, clon, c_sem.at[1]),
             pltpu.make_async_copy(thick_hbm, thick, c_sem.at[2])]
    small[0].start()
    loads[0].start()
    small[1].start()
    for c in loads[1:]:
        c.start()
    small[2].start()

    def peer(k):
        return lax.rem(lev + k, ND)

    bar = pltpu.get_barrier_semaphore()
    for k in range(1, ND):
        pl.semaphore_signal(bar, inc=1, device_id=(lat, peer(k)), device_id_type=MESH)

    @pl.when(lat > 0)
    def _():
        pl.semaphore_signal(bar, inc=1, device_id=(lat - 1, lev), device_id_type=MESH)

    @pl.when(lat < lat_axis - 1)
    def _():
        pl.semaphore_signal(bar, inc=1, device_id=(lat + 1, lev), device_id_type=MESH)

    inner = jnp.where(lat > 0, 1, 0) + jnp.where(lat < lat_axis - 1, 1, 0)
    pl.semaphore_wait(bar, ND - 1 + inner)

    def edge_copy():
        return pltpu.make_async_remote_copy(clat_hbm.at[0], cnorth, hsend.at[2, 0], hrecv.at[2, 0],
                                            device_id=(lat - 1, lev), device_id_type=MESH)

    def to_south(t):
        return pltpu.make_async_remote_copy(x_hbm.at[t, 0:3], north.at[t], hsend.at[0, t], hrecv.at[0, t],
                                            device_id=(lat - 1, lev), device_id_type=MESH)

    def to_north(t):
        return pltpu.make_async_remote_copy(x_hbm.at[t, NI - 3:NI], south.at[t], hsend.at[1, t], hrecv.at[1, t],
                                            device_id=(lat + 1, lev), device_id_type=MESH)

    has_south, has_north = lat > 0, lat < lat_axis - 1

    @pl.when(has_south)
    def _():
        edge_copy().start()

    for t in range(NT):
        @pl.when(has_south)
        def _():
            to_south(t).start()

        @pl.when(has_north)
        def _():
            to_north(t).start()

    @pl.when(lat == 0)
    def _():
        south[...] = jnp.zeros_like(south)

    @pl.when(lat == lat_axis - 1)
    def _():
        north[...] = jnp.zeros_like(north)
        cnorth[...] = jnp.zeros_like(cnorth)

    small[0].wait()
    small[1].wait()

    def weigh(i, _):
        for k, w in enumerate(face_weights(clat[i])):
            wlat[k, i] = w
        for k, w in enumerate(face_weights(clon[i])):
            wlon[k, i] = w
        return 0

    lax.fori_loop(0, NI, weigh, 0)

    def clear(t, _):
        for e in range(ND):
            send[t, e, 112:120, :] = jnp.zeros((8, 128), F32)
        return 0

    lax.fori_loop(0, NT, clear, 0)

    @pl.when(has_north)
    def _():
        edge_copy().wait_recv()

    for k, w in enumerate(face_weights(cnorth[...])):
        wlat[k, NI] = w

    def across(t, k):
        e = peer(k)
        return pltpu.make_async_remote_copy(send.at[t, e], recv.at[lev, t], ssem.at[t, k], rsem.at[t, lev],
                                            device_id=(lat, e), device_id_type=MESH)

    def own(t):
        return pltpu.make_async_copy(send.at[t, lev], recv.at[lev, t], lsem.at[t])

    def forward(t, _):
        pltpu.make_async_copy(x_hbm.at[t], xs.at[t], x_sem.at[t]).wait()

        @pl.when(has_north)
        def _():
            to_south(t).wait_recv()

        @pl.when(has_south)
        def _():
            to_north(t).wait_recv()

        latitude_part(t, xs, south, north, wlat, part)
        longitude_part(t, xs, wlon, part, send)
        for k in ORDER:
            across(t, k).start()
        own(t).start()
        return 0

    lax.fori_loop(0, NT, forward, 0)

    small[2].wait()
    prep(cnt_ref, thick, eta_ref, sl_s, h_s, idx_s, dt_s, rt_s, fr_s, th_s)

    r = lax.broadcasted_iota(jnp.int32, (128, 128), 0)
    l = lax.broadcasted_iota(jnp.int32, (128, 128), 1)
    tri = jnp.where(l < r, 1.0, 0.0)

    def put(t, slot):
        return pltpu.make_async_copy(stage.at[slot], out_hbm.at[t], osem.at[slot])

    def settle(t, _):
        slot = lax.rem(t, 2)

        @pl.when(t >= 2)
        def _():
            put(t - 2, slot).wait()

        own(t).wait()
        for k in range(1, ND):
            src = peer(k)
            pltpu.make_async_remote_copy(send.at[t, src], recv.at[src, t], ssem.at[t, k], rsem.at[t, src],
                                         device_id=(lat, src), device_id_type=MESH).wait_recv()

        def tile(ct, _):
            def q_of(d):
                return recv[d, t, pl.ds(pl.multiple_of(8 * ct, 8), 8), :], recv[d, t, pl.ds(72 + 5 * ct, 8), :]
            res = remap_tile(q_of, ct, h_s, idx_s, dt_s, rt_s, c_s, q_s, f_s, tri)

            @pl.when(ct < NI)
            def _():
                stage[slot, lax.rem(ct, NI), :, 0:128] = res

            @pl.when(ct == NI)
            def _():
                for i in range(NI):
                    stage[slot, i, :, 128:SPAN] = res[:, 16 * i:16 * i + 16]
            return 0

        lax.fori_loop(0, NI + 1, tile, 0)
        put(t, slot).start()
        return 0

    lax.fori_loop(0, NT, settle, 0)
    put(NT - 2, 0).wait()
    put(NT - 1, 1).wait()

    def drain(t, _):
        for k in range(1, ND):
            across(t, k).wait_send()

        @pl.when(has_south)
        def _():
            to_south(t).wait_send()

        @pl.when(has_north)
        def _():
            to_north(t).wait_send()
        return 0

    lax.fori_loop(0, NT, drain, 0)

    @pl.when(has_south)
    def _():
        edge_copy().wait_send()


ORDER = (1, 7, 2, 6, 3, 5, 4)


def shards(tracers, courant_lon, courant_lat, level_counts, thick_source, eta_weights):
    dma, any_ = pltpu.SemaphoreType.DMA, pl.BlockSpec(memory_space=pl.ANY)
    lat_axis, lev_axis = lax.axis_size("lat"), lax.axis_size("lev")
    return pl.pallas_call(
        functools.partial(kernel, lat_axis, lev_axis),
        name="transport",
        out_shape=jax.ShapeDtypeStruct((NT, NI, 72, SPAN), F32),
        in_specs=[pl.BlockSpec(memory_space=pltpu.SMEM), any_, any_, any_, any_, pl.BlockSpec(memory_space=pltpu.VMEM)],
        out_specs=any_,
        scratch_shapes=[
            pltpu.VMEM((NT, NI, NS, NX), F32),
            pltpu.VMEM((NT, 3, NS, NX), F32),
            pltpu.VMEM((NT, 3, NS, NX), F32),
            pltpu.VMEM((NI, NS, NX), F32),
            pltpu.VMEM((NI, NS, NX), F32),
            pltpu.VMEM((NS, NX), F32),
            pltpu.VMEM((3, NI + 1, NS, NX), F32),
            pltpu.VMEM((3, NI, NS, NX), F32),
            pltpu.VMEM((NI, NS, NX), F32),
            pltpu.VMEM((NT, ND, ROWS, 128), F32),
            pltpu.VMEM((ND, NT, ROWS, 128), F32),
            pltpu.VMEM((NI, 72, SPAN), F32),
            pltpu.VMEM((2, NI, 72, SPAN), F32),
            pltpu.VMEM((2, 128, 128), F32),
            pltpu.VMEM((9, 128, 128), F32),
            pltpu.VMEM((9, 72, 128), jnp.int32),
            pltpu.VMEM((9, 72, 128), F32),
            pltpu.VMEM((9, 72, 128), F32),
            pltpu.VMEM((2, 72, 128), F32),
            pltpu.VMEM((9, 72, 128), F32),
            pltpu.VMEM((128, 128), F32),
            pltpu.VMEM((128, 128), F32),
            pltpu.VMEM((80, 128), F32),
            dma((NT,)),
            dma((3,)),
            dma((3, NT)),
            dma((3, NT)),
            dma((NT, ND)),
            dma((NT, ND)),
            dma((NT,)),
            dma((2,)),
        ],
        compiler_params=pltpu.CompilerParams(collective_id=0, has_side_effects=True, vmem_limit_bytes=52 << 20),
    )(level_counts, tracers, courant_lon, courant_lat, thick_source, eta_weights.reshape(1, 72))


def solution(mesh):
    return jax.shard_map(
        shards,
        mesh=mesh,
        in_specs=(
            P(None, "lat", "lev", None),
            P("lat", "lev", None),
            P("lat", "lev", None),
            P(),
            P("lat", None, "lev"),
            P(),
        ),
        out_specs=P(None, "lat", None, "lev"),
        check_vma=False,
    )
```

time: 889 us -> 96.9 us (0.11)
  the two profiles are of different devices: /device:TPU:7 before, /device:TPU:1 now
where the time goes in v1:
time: 96.9 us; the launch traced here: 95.5 us
  Pallas kernels  83 us (86%)
  local copies, waits for them, and re-layouts  12.4 us (13%)
    pallas_call x1, Pallas kernels, shards(): pl.pallas_call(functools.partial(kernel, lat_axis, lev_axis), name='trans...  83 us
    unnamed x10, local copies, waits for them, and re-layouts  12.4 us

profile of v1, /device:TPU:1, one launch (start us, length us, event | category | flops | bytes accessed | tf_op | source)
XLA Modules:
  0.0 95.5 jit_solution(2015460819054228312)
XLA Ops:
  0.0 1.1 %copy.8.clon_hbm = f32[8,13,1152]{2,1,0:T(8,128)S(1)} copy(f32[8,13,1152]{2,0,1:T(8,128)} %param.7) | data formatting | bytes 958464 | tf_op args[1]
  1.1 0.0 copy-start
  1.2 0.0 copy-start.1
  1.2 0.0 copy-start.2
  1.2 1.2 %copy.9.clat_hbm = f32[8,13,1152]{2,1,0:T(8,128)S(1)} copy(f32[8,13,1152]{2,0,1:T(8,128)} %param.8) | data formatting | bytes 958464 | tf_op args[2]
  2.4 5.1 %copy.7.x_hbm = f32[8,8,13,1152]{3,2,1,0:T(8,128)} copy(f32[8,8,13,1152]{3,1,2,0:T(8,128)} %param.6) | data formatting | bytes 7667712 | tf_op args[0]
  7.5 0.0 copy-done
  7.5 0.0 copy-done.1
  7.5 0.0 copy-done.2
  7.5 83.0 %transport.1 = f32[8,8,72,144]{3,2,1,0:T(8,128)} custom-call(s32[8]{0:T(128)S(1)} %copy-done.1, f32[8,8,13,1152]{3,2,1,0:T(8,128)} %copy.7.x_hbm, f32[8,13,1152]{2,1,0:T(8,128)S(1)} %copy.8.clon_hbm, f32[8,13,1152]{2,1,0:T(8,128)S(1)} %copy.9.clat_hbm, f32[8,72,144]{2,1,0:T(8,128)S(1)} %copy-done, f32[1,72]{1,0:T(1,128)S(1)} %bitcast.1), custom_call_target="tpu_custom_call" | custom-call | tf_op jit(solution)/shard_map/transport/pallas_call | solution.py:349
  90.6 4.9 %copy.11 = f32[8,8,72,144]{3,2,1,0:T(8,128)} copy(f32[8,8,72,144]{3,2,1,0:T(8,128)} %transport.1) | data formatting | bytes 5308416
Async XLA Ops:
  1.1 6.4 %copy-start = (f32[8,72,144]{2,1,0:T(8,128)S(1)}, f32[8,72,144]{2,1,0:T(8,128)}, u32[]{:S(2)}) copy-start(f32[8,72,144]{2,1,0:T(8,128)} %thick_hbm.1) | copy-start | bytes 995332
  1.2 6.4 %copy-start.1 = (s32[8]{0:T(128)S(1)}, s32[8]{0:T(128)}, u32[]{:S(2)}) copy-start(s32[8]{0:T(128)} %cnt_ref.1) | copy-start | bytes 100
  1.2 6.3 %copy-start.2 = (f32[72]{0:T(128)S(1)}, f32[72]{0:T(128)}, u32[]{:S(2)}) copy-start(f32[72]{0:T(128)} %param.11) | copy-start | bytes 868

commit v2 on v1

v2 whole, which is shorter than its diff:
```python
import functools
import jax
import jax.numpy as jnp
from jax import lax
from jax.experimental import pallas as pl
from jax.experimental.pallas import tpu as pltpu
from jax.sharding import PartitionSpec as P

MESH = pl.DeviceIdType.MESH
HI = lax.Precision.HIGHEST
F32 = jnp.float32
NT, NI, NS, NX, ND, NK = 8, 8, 13, 1152, 8, 72
SPAN = NX // ND
ROWS = 120
SLOTS = ND * NS
ORDER = (1, 7, 2, 6, 3, 5, 4)


def gather(v, idx, axis):
    return jnp.take_along_axis(v, idx, axis=axis, mode="promise_in_bounds")


def iota(shape, axis):
    return lax.broadcasted_iota(jnp.int32, shape, axis)


def face_weights(c):
    m = jnp.abs(c)
    r = 1.0 - m
    cm = c * m
    return c * r * r * (1.0 / 12.0), cm * (3.0 - 2.0 * m), cm * r * (-1.0 / 12.0)


def flux_of(w, a, behind, ahead, a_behind, a_ahead):
    up = w[0] >= 0.0
    return w[0] * a + w[1] * jnp.where(up, behind, ahead) + w[2] * jnp.where(up, a_behind, a_ahead)


def face(q2, q1, q, qa):
    return 7.0 * (q1 + q) - (q2 + qa)


def edges(t, rows, inner, wedge, edge_s):
    def column(k, _):
        lanes = pl.ds(pl.multiple_of(k * 128, 128), 128)
        for lo, hi in ((0, 8), (8, NS)):
            n0, n1, n2, s3, s2, s1 = [rows[t, j, lo:hi, lanes] for j in range(6)]
            q0, q5, q6, q7 = [inner[t, j, lo:hi, lanes] for j in range(4)]
            a8 = face(q6, q7, n0, n1)
            edge_s[0, lo:hi, lanes] = face(s3, s2, s1, q0)
            edge_s[1, lo:hi, lanes] = a8
            edge_s[2, lo:hi, lanes] = flux_of(
                [wedge[j, lo:hi, lanes] for j in range(3)], a8, q7, n0, face(q5, q6, q7, n0), face(q7, n0, n1, n2))
        return 0

    lax.fori_loop(0, NX // 128, column, 0)


def stencil():
    p, c = iota((4 * 128, 4 * 128), 0), iota((4 * 128, 4 * 128), 1)
    u, kind = p & 127, c >> 7
    at = jnp.where(p < 256, u, jnp.where(u >= 64, u - 128, u + 128)) - (c & 127)
    near = at + jnp.where(kind == 1, 1, jnp.where(kind == 2, -1, 0))
    value = jnp.where((near == -1) | (near == 0), 7.0, jnp.where((near == -2) | (near == 1), -1.0, 0.0))
    return jnp.where(kind == 3, jnp.where(at == -1, 1.0, 0.0), value).astype(jnp.bfloat16)


def halves(v):
    hi = v.astype(jnp.bfloat16)
    return hi, (v - hi.astype(F32)).astype(jnp.bfloat16)


def lane_stencil(t, xs, sten, taps, faces):
    nk = NX // 128
    pad = jnp.zeros((8, 128), F32)
    lane = iota((NS * NI, 128), 1)
    for k in range(nk):
        col = [xs[t, :, :, 128 * j:128 * j + 128].reshape(NS * NI, 128) for j in ((k + nk - 1) % nk, k, (k + 1) % nk)]
        both = halves(jnp.concatenate([col[1], pad], axis=0)) + halves(
            jnp.concatenate([jnp.where(lane >= 64, col[0], col[2]), pad], axis=0))
        for j, piece in enumerate(both):
            taps[112 * k:112 * k + 112, 128 * j:128 * j + 128] = piece
    faces[...] = jnp.dot(taps[...], sten[...], preferred_element_type=F32)


def horizontal(t, xs, rows, edge_s, wlat, wlon, sten, taps, faces, send):
    sub, lane = iota((8, 128), 0), iota((8, 128), 1)
    first, second, last = sub == 0, sub == 1, sub == 7
    nk = NX // 128
    lane_stencil(t, xs, sten, taps, faces)

    def wide(ref, l, k):
        return jnp.broadcast_to(ref[l:l + 1, 128 * k:128 * k + 128], (8, 128))

    for l in range(NS):
        q = [xs[t, l, :, 128 * k:128 * k + 128] for k in range(nk)]
        flux = []
        for k in range(nk):
            a, a_west, a_east, west = [faces[112 * k + 8 * l:112 * k + 8 * l + 8, 128 * j:128 * j + 128] for j in range(4)]
            flux.append(flux_of([wlon[j, l, :, 128 * k:128 * k + 128] for j in range(3)], a, west, q[k], a_west, a_east))
        turned = [pltpu.roll(f, 127, 1) for f in flux]
        h = []
        for k in range(nk):
            s1 = wide(rows.at[t, 5], l, k)
            q1 = jnp.where(first, s1, pltpu.roll(q[k], 1, 0))
            q2 = jnp.where(first, wide(rows.at[t, 4], l, k), jnp.where(second, s1, pltpu.roll(q[k], 2, 0)))
            qa = jnp.where(last, wide(rows.at[t, 0], l, k), pltpu.roll(q[k], 7, 0))
            b = face(q2, q1, q[k], qa)
            b1 = jnp.where(first, wide(edge_s.at[0], l, k), pltpu.roll(b, 1, 0))
            ba = jnp.where(last, wide(edge_s.at[1], l, k), pltpu.roll(b, 7, 0))
            g = flux_of([wlat[j, l, :, 128 * k:128 * k + 128] for j in range(3)], b, q1, q[k], b1, ba)
            ga = jnp.where(last, wide(edge_s.at[2], l, k), pltpu.roll(g, 7, 0))
            flux_east = jnp.where(lane < 127, turned[k], turned[(k + 1) % nk])
            h.append((q[k] - (flux_east - flux[k])) - (ga - g))
        tail, at = 104 + 8 * (l // 8), 16 * (l % 8)
        for e in range(ND):
            send[t, e, 8 * l:8 * l + 8, :] = jnp.where(lane >= 16 * e, h[e], h[e + 1]) if e else h[0]
            turn = (128 - 16 * e + at) % 128
            piece = pltpu.roll(h[e + 1], turn, 1) if turn else h[e + 1]
            send[t, e, tail:tail + 8, at:at + 16] = piece[:, at:at + 16]


def split(v, parts):
    out = []
    for _ in range(parts):
        p = v.astype(jnp.bfloat16)
        out.append(p)
        v = v - p.astype(F32)
    return jnp.concatenate(out, axis=0)


def zero_one(mask, parts):
    return jnp.concatenate([jnp.where(mask, 1.0, 0.0)] * parts, axis=1)


def mul(m, v):
    return jnp.dot(m.astype(jnp.bfloat16), v, preferred_element_type=F32)


def prep(lev, cnt_ref, thick_ref, eta_ref, pick_s, sum_s, su_s, th_s, idx_s, dt_s, rt_s, fr_s):
    for i in range(NI):
        th_s[:, 128 * i:128 * i + 128] = pltpu.roll(thick_ref[i, :, 0:128], lax.rem(16 * lev, 128), 1)
        th_s[:, NX - 128 + 16 * i:NX - 112 + 16 * i] = thick_ref[i, :, 128:SPAN]
    level, slot = iota((NK, SLOTS), 0), iota((NK, SLOTS), 1)
    source = jnp.zeros((NK, SLOTS), jnp.int32)
    start = jnp.int32(0)
    for d in range(ND):
        c = cnt_ref[d]
        source = jnp.where((level >= start) & (level < start + c), level - start + NS * d, source)
        start = start + c
    pick_s[...] = zero_one(source == slot, 2)
    sum_s[...] = zero_one(iota((NK + 8, NK), 1) < iota((NK + 8, NK), 0), 2)
    r72, l72 = iota((NK, NK), 0), iota((NK, NK), 1)
    eb = jnp.broadcast_to(eta_ref[...], (NK, NK))
    tot = jnp.sum(eb, axis=1, keepdims=True)
    cum = jnp.sum(jnp.where(l72 <= r72, eb, 0.0), axis=1, keepdims=True)
    own = jnp.sum(jnp.where(l72 == r72, eb, 0.0), axis=1, keepdims=True)
    fr_s[0] = jnp.broadcast_to(cum / tot, (NK, 128))
    fr_s[1] = jnp.broadcast_to(own / tot, (NK, 128))
    su_s[...] = mul(zero_one(iota((NK + 8, NK), 1) < iota((NK + 8, NK), 0), 3), split(th_s[...], 3))

    def one(ct, _):
        lanes = pl.ds(pl.multiple_of(ct * 128, 128), 128)
        ps = jnp.broadcast_to(su_s[NK:NK + 1, lanes], (8, 128))
        for tb in range(NK // 8):
            at = slice(8 * tb, 8 * tb + 8)
            t = ps * fr_s[0, at, :]
            rt_s[ct, at, :] = 1.0 / (ps * fr_s[1, at, :])
            n = jnp.zeros((8, 128), jnp.int32)
            for r in range(NK):
                n = jnp.where(jnp.broadcast_to(su_s[r + 1:r + 2, lanes], (8, 128)) <= t, r + 1, n)
            loc, vb = n & 7, n >> 3
            g = ps
            gh = jnp.zeros((8, 128), F32)
            for v in range(NK // 8):
                hit = vb == v
                g = jnp.where(hit, gather(su_s[8 * v:8 * v + 8, lanes], loc, 0), g)
                gh = jnp.where(hit, gather(th_s[8 * v:8 * v + 8, lanes], loc, 0), gh)
            idx_s[ct, at, :] = n
            dt_s[ct, at, :] = jnp.clip(t - g, 0.0, gh)
        return 0

    lax.fori_loop(0, NI + 1, one, 0)


def block_turn(p):
    r, l = iota((8, 128), 0), iota((8, 128), 1)
    p = gather(p, (l + 16 * r) & 127, 1)
    p = gather(p, (r - (l >> 4)) & 7, 0)
    return gather(p, ((16 * r - (l & 112)) & 127) + (l & 15), 1)


def remap_tracer(lev, t, slot, recv, stage, pick_s, sum_s, th_s, idx_s, dt_s, rt_s, s_s, q_s, c_s, f_s):
    for d in range(ND):
        a, b = slice(NS * d, NS * d + 8), slice(NS * d + 8, NS * d + NS)
        for ct in range(NI):
            lanes = slice(128 * ct, 128 * ct + 128)
            s_s[a, lanes] = recv[d, t, pl.ds(ct, 8, stride=8), :]
            s_s[b, lanes] = recv[d, t, pl.ds(64 + ct, NS - 8, stride=8), :]
        s_s[a, NX - 128:] = block_turn(recv[d, t, 104:112, :])
        s_s[b, NX - 128:] = block_turn(recv[d, t, 112:120, :])[:NS - 8]
    q_s[...] = mul(pick_s[...], split(s_s[...], 2))
    c_s[...] = mul(sum_s[...], split(q_s[...] * th_s[...], 2))
    f_s[0:8, :] = jnp.zeros((8, 128), F32)

    def tile(ct):
        lanes = pl.ds(ct * 128, 128) if isinstance(ct, int) else pl.ds(pl.multiple_of(ct * 128, 128), 128)
        total = jnp.broadcast_to(c_s[NK:NK + 1, lanes], (8, 128))
        for tb in range(NK // 8):
            at = slice(8 * tb, 8 * tb + 8)
            n = idx_s[ct, at, :]
            loc, vb = n & 7, n >> 3
            gc = total
            gq = jnp.zeros((8, 128), F32)
            for v in range(NK // 8):
                hit = vb == v
                gc = jnp.where(hit, gather(c_s[8 * v:8 * v + 8, lanes], loc, 0), gc)
                gq = jnp.where(hit, gather(q_s[8 * v:8 * v + 8, lanes], loc, 0), gq)
            f_s[8 + 8 * tb:16 + 8 * tb, :] = gc + dt_s[ct, at, :] * gq
        return (f_s[8:80, :] - f_s[7:79, :]) * rt_s[ct]

    def main(ct, _):
        stage[slot, ct, :, 0:128] = pltpu.roll(tile(ct), lax.rem(128 - 16 * lev, 128), 1)
        return 0

    lax.fori_loop(0, NI, main, 0)
    res = tile(NI)
    for i in range(NI):
        stage[slot, i, :, 128:SPAN] = res[:, 16 * i:16 * i + 16]


def kernel(lat_axis, cnt_ref, x_hbm, clon_hbm, clat_hbm, thick_ref, eta_ref, out_ref,
           xs, rows, inner, clon, clat, cnorth, wlat, wedge, wlon, edge_s, sten, taps, faces, send, recv,
           pick_s, sum_s, su_s, th_s, idx_s, dt_s, rt_s, fr_s, s_s, q_s, c_s, f_s,
           x_sem, i_sem, c_sem, esem, hsend, hrecv, ssem, rsem, lsem):
    lat, lev = lax.axis_index("lat"), lax.axis_index("lev")
    has_south, has_north = lat > 0, lat < lat_axis - 1

    small = [pltpu.make_async_copy(clat_hbm, clat, c_sem.at[0]), pltpu.make_async_copy(clon_hbm, clon, c_sem.at[1])]
    loads = [pltpu.make_async_copy(x_hbm.at[t], xs.at[t], x_sem.at[t]) for t in range(NT)]
    def inner_load(t, j):
        return pltpu.make_async_copy(x_hbm.at[t, :, (0, 5, 6, 7)[j], :], inner.at[t, j], i_sem.at[t, j])

    small[0].start()
    small[1].start()
    for t in range(NT):
        loads[t].start()
        for j in range(4):
            inner_load(t, j).start()

    def peer(k):
        return lax.rem(lev + k, ND)

    bar = pltpu.get_barrier_semaphore()
    for k in range(1, ND):
        pl.semaphore_signal(bar, inc=1, device_id=(lat, peer(k)), device_id_type=MESH)

    @pl.when(has_south)
    def _():
        pl.semaphore_signal(bar, inc=1, device_id=(lat - 1, lev), device_id_type=MESH)

    @pl.when(has_north)
    def _():
        pl.semaphore_signal(bar, inc=1, device_id=(lat + 1, lev), device_id_type=MESH)

    others = jnp.where(has_south, 1, 0) + jnp.where(has_north, 1, 0)
    pl.semaphore_wait(bar, ND - 1 + others)

    def edge_copy():
        return pltpu.make_async_remote_copy(clat_hbm.at[:, 0, :], cnorth, esem.at[0], esem.at[1],
                                            device_id=(lat - 1, lev), device_id_type=MESH)

    def to_south(t, j):
        return pltpu.make_async_remote_copy(x_hbm.at[t, :, j, :], rows.at[t, j], hsend.at[t, j], hrecv.at[t, j],
                                            device_id=(lat - 1, lev), device_id_type=MESH)

    def to_north(t, j):
        return pltpu.make_async_remote_copy(x_hbm.at[t, :, 2 + j, :], rows.at[t, j], hsend.at[t, j], hrecv.at[t, j],
                                            device_id=(lat + 1, lev), device_id_type=MESH)

    @pl.when(has_south)
    def _():
        edge_copy().start()

    for t in range(NT):
        @pl.when(has_south)
        def _():
            for j in range(3):
                to_south(t, j).start()

        @pl.when(has_north)
        def _():
            for j in range(3, 6):
                to_north(t, j).start()

    @pl.when(lat == 0)
    def _():
        rows[:, 3:6] = jnp.zeros((NT, 3, NS, NX), F32)

    @pl.when(lat == lat_axis - 1)
    def _():
        rows[:, 0:3] = jnp.zeros((NT, 3, NS, NX), F32)
        cnorth[...] = jnp.zeros_like(cnorth)

    sten[...] = stencil()
    small[0].wait()
    small[1].wait()

    def weigh(l, _):
        for k, w in enumerate(face_weights(clat[l])):
            wlat[k, l] = w
        for k, w in enumerate(face_weights(clon[l])):
            wlon[k, l] = w
        return 0

    lax.fori_loop(0, NS, weigh, 0)

    def clear(t, _):
        for e in range(ND):
            send[t, e, 112:120, :] = jnp.zeros((8, 128), F32)
        return 0

    lax.fori_loop(0, NT, clear, 0)

    @pl.when(has_north)
    def _():
        edge_copy().wait_recv()

    for k, w in enumerate(face_weights(cnorth[...])):
        wedge[k] = w

    def across(t, k):
        e = peer(k)
        return pltpu.make_async_remote_copy(send.at[t, e], recv.at[lev, t], ssem.at[t, k], rsem.at[t, lev],
                                            device_id=(lat, e), device_id_type=MESH)

    def own(t):
        return pltpu.make_async_copy(send.at[t, lev], recv.at[lev, t], lsem.at[t])

    def forward(t, _):
        pltpu.make_async_copy(x_hbm.at[t], xs.at[t], x_sem.at[t]).wait()

        @pl.when(has_north)
        def _():
            for j in range(3):
                to_south(t, j).wait_recv()

        @pl.when(has_south)
        def _():
            for j in range(3, 6):
                to_north(t, j).wait_recv()

        for j in range(4):
            inner_load(t, j).wait()
        edges(t, rows, inner, wedge, edge_s)
        horizontal(t, xs, rows, edge_s, wlat, wlon, sten, taps, faces, send)
        for k in ORDER:
            across(t, k).start()
        own(t).start()
        return 0

    lax.fori_loop(0, NT, forward, 0)

    prep(lev, cnt_ref, thick_ref, eta_ref, pick_s, sum_s, su_s, th_s, idx_s, dt_s, rt_s, fr_s)

    def settle(t, _):
        own(t).wait()
        for k in range(1, ND):
            src = peer(k)
            pltpu.make_async_remote_copy(send.at[t, src], recv.at[src, t], ssem.at[t, k], rsem.at[t, src],
                                         device_id=(lat, src), device_id_type=MESH).wait_recv()
        remap_tracer(lev, t, t, recv, out_ref, pick_s, sum_s, th_s, idx_s, dt_s, rt_s, s_s, q_s, c_s, f_s)
        return 0

    lax.fori_loop(0, NT, settle, 0)

    def drain(t, _):
        for k in range(1, ND):
            across(t, k).wait_send()

        @pl.when(has_south)
        def _():
            for j in range(3):
                to_south(t, j).wait_send()

        @pl.when(has_north)
        def _():
            for j in range(3, 6):
                to_north(t, j).wait_send()
        return 0

    lax.fori_loop(0, NT, drain, 0)

    @pl.when(has_south)
    def _():
        edge_copy().wait_send()


def shards(tracers, courant_lon, courant_lat, level_counts, thick_source, eta_weights):
    dma, any_, vmem = pltpu.SemaphoreType.DMA, pl.BlockSpec(memory_space=pl.ANY), pl.BlockSpec(memory_space=pltpu.VMEM)
    tile9 = pltpu.VMEM((NI + 1, NK, 128), F32)
    return pl.pallas_call(
        functools.partial(kernel, lax.axis_size("lat")),
        name="transport",
        out_shape=jax.ShapeDtypeStruct((NT, NI, NK, SPAN), F32),
        in_specs=[pl.BlockSpec(memory_space=pltpu.SMEM), any_, any_, any_, vmem, vmem],
        out_specs=vmem,
        scratch_shapes=[
            pltpu.VMEM((NT, NS, NI, NX), F32),
            pltpu.VMEM((NT, 6, NS, NX), F32),
            pltpu.VMEM((NT, 4, NS, NX), F32),
            pltpu.VMEM((NS, NI, NX), F32),
            pltpu.VMEM((NS, NI, NX), F32),
            pltpu.VMEM((NS, NX), F32),
            pltpu.VMEM((3, NS, NI, NX), F32),
            pltpu.VMEM((3, NS, NX), F32),
            pltpu.VMEM((3, NS, NI, NX), F32),
            pltpu.VMEM((3, NS, NX), F32),
            pltpu.VMEM((512, 512), jnp.bfloat16),
            pltpu.VMEM((9 * 112, 512), jnp.bfloat16),
            pltpu.VMEM((9 * 112, 512), F32),
            pltpu.VMEM((NT, ND, ROWS, 128), F32),
            pltpu.VMEM((ND, NT, ROWS, 128), F32),
            pltpu.VMEM((NK, 2 * SLOTS), F32),
            pltpu.VMEM((NK + 8, 2 * NK), F32),
            pltpu.VMEM((NK + 8, NX), F32),
            pltpu.VMEM((NK, NX), F32),
            pltpu.VMEM((NI + 1, NK, 128), jnp.int32),
            tile9,
            tile9,
            pltpu.VMEM((2, NK, 128), F32),
            pltpu.VMEM((SLOTS, NX), F32),
            pltpu.VMEM((NK, NX), F32),
            pltpu.VMEM((NK + 8, NX), F32),
            pltpu.VMEM((NK + 8, 128), F32),
            dma((NT,)),
            dma((NT, 4)),
            dma((2,)),
            dma((2,)),
            dma((NT, 6)),
            dma((NT, 6)),
            dma((NT, ND)),
            dma((NT, ND)),
            dma((NT,)),
        ],
        compiler_params=pltpu.CompilerParams(collective_id=0, has_side_effects=True, vmem_limit_bytes=57 << 20),
    )(level_counts, jnp.swapaxes(tracers, 1, 2), jnp.swapaxes(courant_lon, 0, 1), jnp.swapaxes(courant_lat, 0, 1),
      thick_source, eta_weights.reshape(1, NK))


def solution(mesh):
    return jax.shard_map(
        shards,
        mesh=mesh,
        in_specs=(
            P(None, "lat", "lev", None),
            P("lat", "lev", None),
            P("lat", "lev", None),
            P(),
            P("lat", None, "lev"),
            P(),
        ),
        out_specs=P(None, "lat", None, "lev"),
        check_vma=False,
    )
```

time: 96.9 us -> 85.4 us (0.88); the launches traced: 95.5 us -> 85.3 us
  local copies, waits for them, and re-layouts: 12.4 us -> 4.93 us
  Pallas kernels: 83 us -> 80.3 us
    unnamed x10 -> x1, local copies, waits for them, and re-layouts: 12.4 us -> 4.93 us
    pallas_call x1, Pallas kernels: 83 us -> 80.3 us  [shards(): pl.pallas_call(functools.partial(kernel, lax.axis_size('lat')), name='tra...]
where the time goes in v2:
time: 85.4 us; the launch traced here: 85.3 us
  Pallas kernels  80.3 us (94%)
  local copies, waits for them, and re-layouts  4.93 us (6%)
    pallas_call x1, Pallas kernels, shards(): pl.pallas_call(functools.partial(kernel, lax.axis_size('lat')), name='tra...  80.3 us
    unnamed x1, local copies, waits for them, and re-layouts  4.93 us

profile of v2, /device:TPU:1, one launch (start us, length us, event | category | flops | bytes accessed | tf_op | source)
XLA Modules:
  0.0 85.3 jit_solution(12574274480286082931)
XLA Ops:
  0.0 80.3 %transport.1 = f32[8,8,72,144]{3,2,1,0:T(8,128)} custom-call(s32[8]{0:T(128)} %cnt_ref.1, f32[8,13,8,1152]{3,2,1,0:T(8,128)} %bitcast.4, f32[13,8,1152]{2,1,0:T(8,128)} %bitcast.5, f32[13,8,1152]{2,1,0:T(8,128)} %bitcast.6, f32[8,72,144]{2,1,0:T(8,128)} %thick_ref.1, f32[1,72]{1,0:T(1,128)} %bitcast.7), custom_call_target="tpu_custom_call" | custom-call | tf_op jit(solution)/shard_map/transport/pallas_call | solution.py:402
  80.3 4.9 %copy.8 = f32[8,8,72,144]{3,2,1,0:T(8,128)} copy(f32[8,8,72,144]{3,2,1,0:T(8,128)} %transport.1) | data formatting | bytes 5308416

commit v3 on v2

--- a/solution.py
+++ b/solution.py
@@ -13,6 +13,7 @@
 SPAN = NX // ND
 ROWS = 120
 SLOTS = ND * NS
+LINES = 4
 ORDER = (1, 7, 2, 6, 3, 5, 4)
 
 
@@ -230,9 +231,9 @@
 
 
 def kernel(lat_axis, cnt_ref, x_hbm, clon_hbm, clat_hbm, thick_ref, eta_ref, out_ref,
-           xs, rows, inner, clon, clat, cnorth, wlat, wedge, wlon, edge_s, sten, taps, faces, send, recv,
+           xs, rows, inner, clon, clat, cnorth, wlat, wedge, wlon, edge_s, sten, taps, faces, held, send, recv,
            pick_s, sum_s, su_s, th_s, idx_s, dt_s, rt_s, fr_s, s_s, q_s, c_s, f_s,
-           x_sem, i_sem, c_sem, esem, hsend, hrecv, ssem, rsem, lsem):
+           x_sem, i_sem, c_sem, esem, hsend, hrecv, held_sem, rest_sem, ssem, rsem, lsem):
     lat, lev = lax.axis_index("lat"), lax.axis_index("lev")
     has_south, has_north = lat > 0, lat < lat_axis - 1
 
@@ -263,7 +264,26 @@
     def _():
         pl.semaphore_signal(bar, inc=1, device_id=(lat + 1, lev), device_id_type=MESH)
 
-    others = jnp.where(has_south, 1, 0) + jnp.where(has_north, 1, 0)
+    below, above = lat_axis // 2 - 1, lat_axis // 2
+    up_relays = [lat_axis - 2 * i for i in range(1, LINES)]
+    down_relays = [2 * i - 1 for i in range(1, LINES)]
+
+    def one_of(places):
+        return functools.reduce(jnp.logical_or, [lat == p for p in places])
+
+    def greet(here, places):
+        @pl.when(here)
+        def _():
+            for p in places:
+                pl.semaphore_signal(bar, inc=1, device_id=(p, lev), device_id_type=MESH)
+
+    is_up, is_down = one_of(up_relays), one_of(down_relays)
+    greet(lat == above, up_relays)
+    greet(lat == below, down_relays)
+    greet(is_up, [below])
+    greet(is_down, [above])
+    others = (jnp.where(has_south, 1, 0) + jnp.where(has_north, 1, 0) + jnp.where(is_up, 1, 0) + jnp.where(is_down, 1, 0)
+              + jnp.where(lat == above, LINES - 1, 0) + jnp.where(lat == below, LINES - 1, 0))
     pl.semaphore_wait(bar, ND - 1 + others)
 
     def edge_copy():
@@ -282,16 +302,62 @@
     def _():
         edge_copy().start()
 
+    def up_leg(t, j):
+        slot = t // LINES
+        return pltpu.make_async_remote_copy(x_hbm.at[t, :, 5 + j, :], held.at[slot, j], hsend.at[t, 3 + j], held_sem.at[slot, j],
+                                            device_id=(lat_axis - 2 * (t % LINES), lev), device_id_type=MESH)
+
+    def down_leg(t, j):
+        slot = t // LINES
+        return pltpu.make_async_remote_copy(x_hbm.at[t, :, j, :], held.at[slot, j], hsend.at[t, j], held_sem.at[slot, j],
+                                            device_id=(2 * (t % LINES) - 1, lev), device_id_type=MESH)
+
+    def up_rest(t, j):
+        return pltpu.make_async_remote_copy(held.at[t // LINES, j], rows.at[t, 3 + j], rest_sem.at[t // LINES, j], hrecv.at[t, 3 + j],
+                                            device_id=(above, lev), device_id_type=MESH)
+
+    def down_rest(t, j):
+        return pltpu.make_async_remote_copy(held.at[t // LINES, j], rows.at[t, j], rest_sem.at[t // LINES, j], hrecv.at[t, j],
+                                            device_id=(below, lev), device_id_type=MESH)
+
+    def relay(t):
+        line = lax.rem(t, LINES)
+
+        @pl.when((t < NT) & (line > 0) & (lat == lat_axis - 2 * line))
+        def _():
+            for j in range(3):
+                up_leg(t, j).wait_recv()
+                up_rest(t, j).start()
+
+        @pl.when((t < NT) & (line > 0) & (lat == 2 * line - 1))
+        def _():
+            for j in range(3):
+                down_leg(t, j).wait_recv()
+                down_rest(t, j).start()
+
     for t in range(NT):
-        @pl.when(has_south)
+        straight = t % LINES == 0
+
+        @pl.when(has_south if straight else has_south & (lat != above))
         def _():
             for j in range(3):
                 to_south(t, j).start()
 
-        @pl.when(has_north)
+        @pl.when(has_north if straight else has_north & (lat != below))
         def _():
             for j in range(3, 6):
                 to_north(t, j).start()
+
+        if not straight:
+            @pl.when(lat == above)
+            def _():
+                for j in range(3):
+                    down_leg(t, j).start()
+
+            @pl.when(lat == below)
+            def _():
+                for j in range(3):
+                    up_leg(t, j).start()
 
     @pl.when(lat == 0)
     def _():
@@ -338,17 +404,31 @@
         return pltpu.make_async_copy(send.at[t, lev], recv.at[lev, t], lsem.at[t])
 
     def forward(t, _):
+        relay(t + 1)
         pltpu.make_async_copy(x_hbm.at[t], xs.at[t], x_sem.at[t]).wait()
 
-        @pl.when(has_north)
+        bent = lax.rem(t, LINES) > 0
+        from_above, from_below = bent & (lat == below), bent & (lat == above)
+
+        @pl.when(has_north & ~from_above)
         def _():
             for j in range(3):
                 to_south(t, j).wait_recv()
 
-        @pl.when(has_south)
+        @pl.when(has_south & ~from_below)
         def _():
             for j in range(3, 6):
                 to_north(t, j).wait_recv()
+
+        @pl.when(from_above)
+        def _():
+            for j in range(3):
+                down_rest(t, j).wait_recv()
+
+        @pl.when(from_below)
+        def _():
+            for j in range(3):
+                up_rest(t, j).wait_recv()
 
         for j in range(4):
             inner_load(t, j).wait()
@@ -390,6 +470,12 @@
         return 0
 
     lax.fori_loop(0, NT, drain, 0)
+
+    @pl.when(is_up | is_down)
+    def _():
+        for slot in range(NT // LINES):
+            for j in range(3):
+                up_rest(slot * LINES, j).wait_send()
 
     @pl.when(has_south)
     def _():
@@ -419,6 +505,7 @@
             pltpu.VMEM((512, 512), jnp.bfloat16),
             pltpu.VMEM((9 * 112, 512), jnp.bfloat16),
             pltpu.VMEM((9 * 112, 512), F32),
+            pltpu.VMEM((NT // LINES, 3, NS, NX), F32),
             pltpu.VMEM((NT, ND, ROWS, 128), F32),
             pltpu.VMEM((ND, NT, ROWS, 128), F32),
             pltpu.VMEM((NK, 2 * SLOTS), F32),
@@ -439,6 +526,8 @@
             dma((2,)),
             dma((NT, 6)),
             dma((NT, 6)),
+            dma((NT // LINES, 3)),
+            dma((NT // LINES, 3)),
             dma((NT, ND)),
             dma((NT, ND)),
             dma((NT,)),

time: 85.4 us -> 74.7 us (0.87)
  the two profiles are of different devices: /device:TPU:1 before, /device:TPU:27 now
where the time goes in v3:
time: 74.7 us; the launch traced here: 74.5 us
  Pallas kernels  69.6 us (93%)
  local copies, waits for them, and re-layouts  4.93 us (7%)
    pallas_call x1, Pallas kernels, shards(): pl.pallas_call(functools.partial(kernel, lax.axis_size('lat')), name='tra...  69.6 us
    unnamed x1, local copies, waits for them, and re-layouts  4.93 us

profile of v3, /device:TPU:27, one launch (start us, length us, event | category | flops | bytes accessed | tf_op | source)
XLA Modules:
  0.0 74.5 jit_solution(3971562527788509521)
XLA Ops:
  0.0 69.6 %transport.1 = f32[8,8,72,144]{3,2,1,0:T(8,128)} custom-call(s32[8]{0:T(128)} %cnt_ref.1, f32[8,13,8,1152]{3,2,1,0:T(8,128)} %bitcast.4, f32[13,8,1152]{2,1,0:T(8,128)} %bitcast.5, f32[13,8,1152]{2,1,0:T(8,128)} %bitcast.6, f32[8,72,144]{2,1,0:T(8,128)} %thick_ref.1, f32[1,72]{1,0:T(1,128)} %bitcast.7), custom_call_target="tpu_custom_call" | custom-call | tf_op jit(solution)/shard_map/transport/pallas_call | solution.py:488
  69.6 4.9 %copy.8 = f32[8,8,72,144]{3,2,1,0:T(8,128)} copy(f32[8,8,72,144]{3,2,1,0:T(8,128)} %transport.1) | data formatting | bytes 5308416

commit v4 on v3

--- a/solution.py
+++ b/solution.py
@@ -13,7 +13,9 @@
 SPAN = NX // ND
 ROWS = 120
 SLOTS = ND * NS
-LINES = 4
+LINES = 3
+HELD = -(-NT // LINES)
+VMEM1, VMEM2 = 57, 57
 ORDER = (1, 7, 2, 6, 3, 5, 4)
 
 
@@ -41,12 +43,12 @@
     return 7.0 * (q1 + q) - (q2 + qa)
 
 
-def edges(t, rows, inner, wedge, edge_s):
+def edges(t, rows, xs, wedge, edge_s):
     def column(k, _):
         lanes = pl.ds(pl.multiple_of(k * 128, 128), 128)
         for lo, hi in ((0, 8), (8, NS)):
             n0, n1, n2, s3, s2, s1 = [rows[t, j, lo:hi, lanes] for j in range(6)]
-            q0, q5, q6, q7 = [inner[t, j, lo:hi, lanes] for j in range(4)]
+            q0, q5, q6, q7 = [xs[t, lo:hi, j, lanes] for j in (0, 5, 6, 7)]
             a8 = face(q6, q7, n0, n1)
             edge_s[0, lo:hi, lanes] = face(s3, s2, s1, q0)
             edge_s[1, lo:hi, lanes] = a8
@@ -134,6 +136,10 @@
     return jnp.concatenate([jnp.where(mask, 1.0, 0.0)] * parts, axis=1)
 
 
+def below_sum():
+    return zero_one(iota((NK + 8, NK), 1) < iota((NK + 8, NK), 0), 2)
+
+
 def mul(m, v):
     return jnp.dot(m.astype(jnp.bfloat16), v, preferred_element_type=F32)
 
@@ -150,7 +156,7 @@
         source = jnp.where((level >= start) & (level < start + c), level - start + NS * d, source)
         start = start + c
     pick_s[...] = zero_one(source == slot, 2)
-    sum_s[...] = zero_one(iota((NK + 8, NK), 1) < iota((NK + 8, NK), 0), 2)
+    sum_s[...] = below_sum()
     r72, l72 = iota((NK, NK), 0), iota((NK, NK), 1)
     eb = jnp.broadcast_to(eta_ref[...], (NK, NK))
     tot = jnp.sum(eb, axis=1, keepdims=True)
@@ -191,7 +197,7 @@
     return gather(p, ((16 * r - (l & 112)) & 127) + (l & 15), 1)
 
 
-def remap_tracer(lev, t, slot, recv, stage, pick_s, sum_s, th_s, idx_s, dt_s, rt_s, s_s, q_s, c_s, f_s):
+def remap_tracer(lev, t, slot, recv, stage, pick_s, sum_s, th_s, idx_s, dt_s, rt_s, s_s, q_s, c_s, f_s, beside=None):
     for d in range(ND):
         a, b = slice(NS * d, NS * d + 8), slice(NS * d + 8, NS * d + NS)
         for ct in range(NI):
@@ -221,6 +227,8 @@
         return (f_s[8:80, :] - f_s[7:79, :]) * rt_s[ct]
 
     def main(ct, _):
+        if beside is not None:
+            beside(ct)
         stage[slot, ct, :, 0:128] = pltpu.roll(tile(ct), lax.rem(128 - 16 * lev, 128), 1)
         return 0
 
@@ -230,24 +238,18 @@
         stage[slot, i, :, 128:SPAN] = res[:, 16 * i:16 * i + 16]
 
 
-def kernel(lat_axis, cnt_ref, x_hbm, clon_hbm, clat_hbm, thick_ref, eta_ref, out_ref,
-           xs, rows, inner, clon, clat, cnorth, wlat, wedge, wlon, edge_s, sten, taps, faces, held, send, recv,
-           pick_s, sum_s, su_s, th_s, idx_s, dt_s, rt_s, fr_s, s_s, q_s, c_s, f_s,
-           x_sem, i_sem, c_sem, esem, hsend, hrecv, held_sem, rest_sem, ssem, rsem, lsem):
+def kernel(lat_axis, cnt_ref, x_hbm, clon_hbm, clat_hbm, thick_ref, eta_ref, done, late, pick_o, th_o, idx_o, dt_o, rt_o,
+           xs, rows, clon, clat, cnorth, wlat, wedge, wlon, edge_s, sten, taps, faces, held, send, recv,
+           pick_s, sum_s, su_s, th_s, idx_s, dt_s, rt_s, fr_s, s_s, q_s, c_s, f_s, stage,
+           x_sem, c_sem, esem, hsend, hrecv, held_sem, rest_sem, ssem, rsem, lsem, psem, osem):
     lat, lev = lax.axis_index("lat"), lax.axis_index("lev")
     has_south, has_north = lat > 0, lat < lat_axis - 1
 
     small = [pltpu.make_async_copy(clat_hbm, clat, c_sem.at[0]), pltpu.make_async_copy(clon_hbm, clon, c_sem.at[1])]
     loads = [pltpu.make_async_copy(x_hbm.at[t], xs.at[t], x_sem.at[t]) for t in range(NT)]
-    def inner_load(t, j):
-        return pltpu.make_async_copy(x_hbm.at[t, :, (0, 5, 6, 7)[j], :], inner.at[t, j], i_sem.at[t, j])
-
     small[0].start()
     small[1].start()
-    for t in range(NT):
-        loads[t].start()
-        for j in range(4):
-            inner_load(t, j).start()
+    loads[0].start()
 
     def peer(k):
         return lax.rem(lev + k, ND)
@@ -359,6 +361,9 @@
                 for j in range(3):
                     up_leg(t, j).start()
 
+        if t > 0:
+            loads[t].start()
+
     @pl.when(lat == 0)
     def _():
         rows[:, 3:6] = jnp.zeros((NT, 3, NS, NX), F32)
@@ -395,13 +400,13 @@
     for k, w in enumerate(face_weights(cnorth[...])):
         wedge[k] = w
 
-    def across(t, k):
+    def across(t, k, last=False):
         e = peer(k)
-        return pltpu.make_async_remote_copy(send.at[t, e], recv.at[lev, t], ssem.at[t, k], rsem.at[t, lev],
+        return pltpu.make_async_remote_copy(send.at[t, e], late.at[lev] if last else recv.at[lev, t], ssem.at[t, k], rsem.at[t, lev],
                                             device_id=(lat, e), device_id_type=MESH)
 
-    def own(t):
-        return pltpu.make_async_copy(send.at[t, lev], recv.at[lev, t], lsem.at[t])
+    def own(t, last=False):
+        return pltpu.make_async_copy(send.at[t, lev], late.at[lev] if last else recv.at[lev, t], lsem.at[t])
 
     def forward(t, _):
         relay(t + 1)
@@ -430,18 +435,33 @@
             for j in range(3):
                 up_rest(t, j).wait_recv()
 
-        for j in range(4):
-            inner_load(t, j).wait()
-        edges(t, rows, inner, wedge, edge_s)
+        edges(t, rows, xs, wedge, edge_s)
         horizontal(t, xs, rows, edge_s, wlat, wlon, sten, taps, faces, send)
-        for k in ORDER:
-            across(t, k).start()
-        own(t).start()
+
+        @pl.when(t < NT - 1)
+        def _():
+            for k in ORDER:
+                across(t, k).start()
+            own(t).start()
+
+        @pl.when(t == NT - 1)
+        def _():
+            for k in ORDER:
+                across(t, k, True).start()
+            own(t, True).start()
         return 0
 
     lax.fori_loop(0, NT, forward, 0)
 
     prep(lev, cnt_ref, thick_ref, eta_ref, pick_s, sum_s, su_s, th_s, idx_s, dt_s, rt_s, fr_s)
+
+    kept = [pltpu.make_async_copy(v, o, psem.at[i]) for i, (v, o) in enumerate(
+        ((pick_s, pick_o), (th_s, th_o), (idx_s, idx_o), (dt_s, dt_o), (rt_s, rt_o)))]
+    for c in kept:
+        c.start()
+
+    def put(t, slot):
+        return pltpu.make_async_copy(stage.at[slot], done.at[t], osem.at[slot])
 
     def settle(t, _):
         own(t).wait()
@@ -449,10 +469,26 @@
             src = peer(k)
             pltpu.make_async_remote_copy(send.at[t, src], recv.at[src, t], ssem.at[t, k], rsem.at[t, src],
                                          device_id=(lat, src), device_id_type=MESH).wait_recv()
-        remap_tracer(lev, t, t, recv, out_ref, pick_s, sum_s, th_s, idx_s, dt_s, rt_s, s_s, q_s, c_s, f_s)
-        return 0
-
-    lax.fori_loop(0, NT, settle, 0)
+        slot = lax.rem(t, 2)
+
+        @pl.when(t >= 2)
+        def _():
+            put(t - 2, slot).wait()
+
+        remap_tracer(lev, t, slot, recv, stage, pick_s, sum_s, th_s, idx_s, dt_s, rt_s, s_s, q_s, c_s, f_s)
+        put(t, slot).start()
+        return 0
+
+    lax.fori_loop(0, NT - 1, settle, 0)
+    put(NT - 3, (NT - 3) % 2).wait()
+    put(NT - 2, (NT - 2) % 2).wait()
+    for c in kept:
+        c.wait()
+    own(NT - 1, True).wait()
+    for k in range(1, ND):
+        src = peer(k)
+        pltpu.make_async_remote_copy(send.at[NT - 1, src], late.at[src], ssem.at[NT - 1, k], rsem.at[NT - 1, src],
+                                     device_id=(lat, src), device_id_type=MESH).wait_recv()
 
     def drain(t, _):
         for k in range(1, ND):
@@ -471,30 +507,70 @@
 
     lax.fori_loop(0, NT, drain, 0)
 
-    @pl.when(is_up | is_down)
-    def _():
-        for slot in range(NT // LINES):
-            for j in range(3):
-                up_rest(slot * LINES, j).wait_send()
+    for t in range(NT):
+        line = t % LINES
+        if line:
+            @pl.when((lat == lat_axis - 2 * line) | (lat == 2 * line - 1))
+            def _():
+                for j in range(3):
+                    up_rest(t, j).wait_send()
 
     @pl.when(has_south)
     def _():
         edge_copy().wait_send()
 
 
+def finish(done, late, pick_h, th_h, idx_h, dt_h, rt_h, out, recv, pick_s, sum_s, th_s, idx_s, dt_s, rt_s, s_s, q_s, c_s, f_s, stage,
+           isem, csem, osem):
+    loads = [pltpu.make_async_copy(h, v, isem.at[i]) for i, (h, v) in enumerate(
+        ((late, recv.at[:, 0]), (pick_h, pick_s), (th_h, th_s), (idx_h, idx_s), (dt_h, dt_s), (rt_h, rt_s)))]
+
+    def fetch(t):
+        return pltpu.make_async_copy(done.at[t], stage.at[t], csem.at[t])
+
+    def write(t):
+        return pltpu.make_async_copy(stage.at[t], out.at[t], osem.at[t])
+
+    def lay_down(t):
+        @pl.when(t < NT - 1)
+        def _():
+            fetch(t).wait()
+            write(t).start()
+
+    for c in loads:
+        c.start()
+    for t in range(NT - 1):
+        fetch(t).start()
+    sum_s[...] = below_sum()
+    for c in loads:
+        c.wait()
+    remap_tracer(lax.axis_index("lev"), 0, NT - 1, recv, stage, pick_s, sum_s, th_s, idx_s, dt_s, rt_s, s_s, q_s, c_s, f_s, lay_down)
+    write(NT - 1).start()
+    for t in range(NT):
+        write(t).wait()
+
+
 def shards(tracers, courant_lon, courant_lat, level_counts, thick_source, eta_weights):
     dma, any_, vmem = pltpu.SemaphoreType.DMA, pl.BlockSpec(memory_space=pl.ANY), pl.BlockSpec(memory_space=pltpu.VMEM)
     tile9 = pltpu.VMEM((NI + 1, NK, 128), F32)
-    return pl.pallas_call(
+    pick = pltpu.VMEM((NK, 2 * SLOTS), F32)
+    sums = pltpu.VMEM((NK + 8, 2 * NK), F32)
+    thick, places = pltpu.VMEM((NK, NX), F32), pltpu.VMEM((NI + 1, NK, 128), jnp.int32)
+    stage = pltpu.VMEM((2, NI, NK, SPAN), F32)
+
+    def shape(v):
+        return jax.ShapeDtypeStruct(v.shape, v.dtype)
+
+    parts = pl.pallas_call(
         functools.partial(kernel, lax.axis_size("lat")),
         name="transport",
-        out_shape=jax.ShapeDtypeStruct((NT, NI, NK, SPAN), F32),
+        out_shape=(jax.ShapeDtypeStruct((NT - 1, NI, NK, SPAN), F32), jax.ShapeDtypeStruct((ND, ROWS, 128), F32),
+                   shape(pick), shape(thick), shape(places), shape(tile9), shape(tile9)),
         in_specs=[pl.BlockSpec(memory_space=pltpu.SMEM), any_, any_, any_, vmem, vmem],
-        out_specs=vmem,
+        out_specs=(any_,) * 7,
         scratch_shapes=[
             pltpu.VMEM((NT, NS, NI, NX), F32),
             pltpu.VMEM((NT, 6, NS, NX), F32),
-            pltpu.VMEM((NT, 4, NS, NX), F32),
             pltpu.VMEM((NS, NI, NX), F32),
             pltpu.VMEM((NS, NI, NX), F32),
             pltpu.VMEM((NS, NX), F32),
@@ -505,14 +581,14 @@
             pltpu.VMEM((512, 512), jnp.bfloat16),
             pltpu.VMEM((9 * 112, 512), jnp.bfloat16),
             pltpu.VMEM((9 * 112, 512), F32),
-            pltpu.VMEM((NT // LINES, 3, NS, NX), F32),
+            pltpu.VMEM((HELD, 3, NS, NX), F32),
             pltpu.VMEM((NT, ND, ROWS, 128), F32),
             pltpu.VMEM((ND, NT, ROWS, 128), F32),
-            pltpu.VMEM((NK, 2 * SLOTS), F32),
-            pltpu.VMEM((NK + 8, 2 * NK), F32),
+            pick,
+            sums,
             pltpu.VMEM((NK + 8, NX), F32),
-            pltpu.VMEM((NK, NX), F32),
-            pltpu.VMEM((NI + 1, NK, 128), jnp.int32),
+            thick,
+            places,
             tile9,
             tile9,
             pltpu.VMEM((2, NK, 128), F32),
@@ -520,21 +596,36 @@
             pltpu.VMEM((NK, NX), F32),
             pltpu.VMEM((NK + 8, NX), F32),
             pltpu.VMEM((NK + 8, 128), F32),
+            stage,
             dma((NT,)),
-            dma((NT, 4)),
             dma((2,)),
             dma((2,)),
             dma((NT, 6)),
             dma((NT, 6)),
-            dma((NT // LINES, 3)),
-            dma((NT // LINES, 3)),
+            dma((HELD, 3)),
+            dma((HELD, 3)),
             dma((NT, ND)),
             dma((NT, ND)),
             dma((NT,)),
+            dma((5,)),
+            dma((2,)),
         ],
-        compiler_params=pltpu.CompilerParams(collective_id=0, has_side_effects=True, vmem_limit_bytes=57 << 20),
+        compiler_params=pltpu.CompilerParams(collective_id=0, has_side_effects=True, vmem_limit_bytes=VMEM1 << 20),
     )(level_counts, jnp.swapaxes(tracers, 1, 2), jnp.swapaxes(courant_lon, 0, 1), jnp.swapaxes(courant_lat, 0, 1),
       thick_source, eta_weights.reshape(1, NK))
+    return pl.pallas_call(
+        finish,
+        name="finish",
+        out_shape=jax.ShapeDtypeStruct((NT, NI, NK, SPAN), F32),
+        in_specs=[any_] * 7,
+        out_specs=any_,
+        scratch_shapes=[
+            pltpu.VMEM((ND, 1, ROWS, 128), F32), pick, sums, thick, places, tile9, tile9,
+            pltpu.VMEM((SLOTS, NX), F32), pltpu.VMEM((NK, NX), F32), pltpu.VMEM((NK + 8, NX), F32), pltpu.VMEM((NK + 8, 128), F32),
+            pltpu.VMEM((NT, NI, NK, SPAN), F32), dma((6,)), dma((NT - 1,)), dma((NT,)),
+        ],
+        compiler_params=pltpu.CompilerParams(vmem_limit_bytes=VMEM2 << 20),
+    )(*parts)
 
 
 def solution(mesh):

time: 74.7 us -> 69.3 us (0.928)
  the two profiles are of different devices: /device:TPU:27 before, /device:TPU:1 now
where the time goes in v4:
time: 69.3 us; the launch traced here: 69.2 us
  Pallas kernels  69.2 us (100%)
    pallas_call x1, Pallas kernels, shards(): pl.pallas_call(functools.partial(kernel, lax.axis_size('lat')), name='tra...  63.7 us
    pallas_call x1, Pallas kernels, shards(): pl.pallas_call(finish, name='finish', out_shape=jax.ShapeDtypeStruct((NT,...  5.51 us

profile of v4, /device:TPU:1, one launch (start us, length us, event | category | flops | bytes accessed | tf_op | source)
XLA Modules:
  0.0 69.2 jit_solution(7485110560452729215)
XLA Ops:
  0.0 63.7 %transport.1 = (f32[7,8,72,144]{3,2,1,0:T(8,128)}, f32[8,120,128]{2,1,0:T(8,128)}, f32[72,208]{1,0:T(8,128)}, f32[72,1152]{1,0:T(8,128)}, s32[9,72,128]{2,1,0:T(...) custom-call(s32[8]{0:T(128)} %cnt_ref.1, f32[8,13,8,1152]{3,2,1,0:T(8,128)} %bitcast.4, f32[13,8,1152]{2,1,0:T(8,128)} %bitcast.5, ...), custom_call_target="tpu_custom_call" | custom-call | tf_op jit(solution)/shard_map/transport/pallas_call | solution.py:564
  63.7 5.5 %finish.1 = f32[8,8,72,144]{3,2,1,0:T(8,128)} custom-call(f32[7,8,72,144]{3,2,1,0:T(8,128)} %get-tuple-element.12.done, f32[8,120,128]{2,1,0:T(8,128)} %get-tuple-element.13.late, f32[72,208]{1,0:T(8,128)} %get-tuple-element.14.pick_h, f32[72,1152]{1,0:T(8,128)} %get-tuple-element.15.th_h, s32[9,72,128]{2,1,0:T(8,128)} %get-tuple-element.16.idx_h, ...), custom_call_target="tpu_custom_call" | custom-call | tf_op jit(solution)/shard_map/finish/pallas_call | solution.py:616

commit v5 on v4

--- a/solution.py
+++ b/solution.py
@@ -11,7 +11,7 @@
 F32 = jnp.float32
 NT, NI, NS, NX, ND, NK = 8, 8, 13, 1152, 8, 72
 SPAN = NX // ND
-ROWS = 120
+ROWS, HEAD = 120, 72
 SLOTS = ND * NS
 LINES = 3
 HELD = -(-NT // LINES)
@@ -86,38 +86,46 @@
     faces[...] = jnp.dot(taps[...], sten[...], preferred_element_type=F32)
 
 
-def horizontal(t, xs, rows, edge_s, wlat, wlon, sten, taps, faces, send):
-    sub, lane = iota((8, 128), 0), iota((8, 128), 1)
-    first, second, last = sub == 0, sub == 1, sub == 7
+def longitude(t, xs, wlon, sten, taps, faces, part):
+    lane = iota((8, 128), 1)
     nk = NX // 128
     lane_stencil(t, xs, sten, taps, faces)
-
-    def wide(ref, l, k):
-        return jnp.broadcast_to(ref[l:l + 1, 128 * k:128 * k + 128], (8, 128))
-
     for l in range(NS):
-        q = [xs[t, l, :, 128 * k:128 * k + 128] for k in range(nk)]
         flux = []
         for k in range(nk):
             a, a_west, a_east, west = [faces[112 * k + 8 * l:112 * k + 8 * l + 8, 128 * j:128 * j + 128] for j in range(4)]
-            flux.append(flux_of([wlon[j, l, :, 128 * k:128 * k + 128] for j in range(3)], a, west, q[k], a_west, a_east))
+            flux.append(flux_of([wlon[j, l, :, 128 * k:128 * k + 128] for j in range(3)], a, west,
+                                xs[t, l, :, 128 * k:128 * k + 128], a_west, a_east))
         turned = [pltpu.roll(f, 127, 1) for f in flux]
+        for k in range(nk):
+            flux_east = jnp.where(lane < 127, turned[k], turned[(k + 1) % nk])
+            part[l, :, 128 * k:128 * k + 128] = xs[t, l, :, 128 * k:128 * k + 128] - (flux_east - flux[k])
+
+
+def latitude(t, levels, xs, rows, edge_s, wlat, part, send):
+    sub, lane = iota((8, 128), 0), iota((8, 128), 1)
+    first, second, last = sub == 0, sub == 1, sub == 7
+
+    def wide(ref, l, k):
+        return jnp.broadcast_to(ref[l:l + 1, 128 * k:128 * k + 128], (8, 128))
+
+    for l in levels:
         h = []
-        for k in range(nk):
+        for k in range(NX // 128):
+            q = xs[t, l, :, 128 * k:128 * k + 128]
             s1 = wide(rows.at[t, 5], l, k)
-            q1 = jnp.where(first, s1, pltpu.roll(q[k], 1, 0))
-            q2 = jnp.where(first, wide(rows.at[t, 4], l, k), jnp.where(second, s1, pltpu.roll(q[k], 2, 0)))
-            qa = jnp.where(last, wide(rows.at[t, 0], l, k), pltpu.roll(q[k], 7, 0))
-            b = face(q2, q1, q[k], qa)
+            q1 = jnp.where(first, s1, pltpu.roll(q, 1, 0))
+            q2 = jnp.where(first, wide(rows.at[t, 4], l, k), jnp.where(second, s1, pltpu.roll(q, 2, 0)))
+            qa = jnp.where(last, wide(rows.at[t, 0], l, k), pltpu.roll(q, 7, 0))
+            b = face(q2, q1, q, qa)
             b1 = jnp.where(first, wide(edge_s.at[0], l, k), pltpu.roll(b, 1, 0))
             ba = jnp.where(last, wide(edge_s.at[1], l, k), pltpu.roll(b, 7, 0))
-            g = flux_of([wlat[j, l, :, 128 * k:128 * k + 128] for j in range(3)], b, q1, q[k], b1, ba)
+            g = flux_of([wlat[j, l, :, 128 * k:128 * k + 128] for j in range(3)], b, q1, q, b1, ba)
             ga = jnp.where(last, wide(edge_s.at[2], l, k), pltpu.roll(g, 7, 0))
-            flux_east = jnp.where(lane < 127, turned[k], turned[(k + 1) % nk])
-            h.append((q[k] - (flux_east - flux[k])) - (ga - g))
-        tail, at = 104 + 8 * (l // 8), 16 * (l % 8)
+            h.append(part[l, :, 128 * k:128 * k + 128] - (ga - g))
+        main, tail, at = 8 * l + (8 if l >= 8 else 0), 112 if l >= 8 else 64, 16 * (l % 8)
         for e in range(ND):
-            send[t, e, 8 * l:8 * l + 8, :] = jnp.where(lane >= 16 * e, h[e], h[e + 1]) if e else h[0]
+            send[t, e, main:main + 8, :] = jnp.where(lane >= 16 * e, h[e], h[e + 1]) if e else h[0]
             turn = (128 - 16 * e + at) % 128
             piece = pltpu.roll(h[e + 1], turn, 1) if turn else h[e + 1]
             send[t, e, tail:tail + 8, at:at + 16] = piece[:, at:at + 16]
@@ -203,8 +211,8 @@
         for ct in range(NI):
             lanes = slice(128 * ct, 128 * ct + 128)
             s_s[a, lanes] = recv[d, t, pl.ds(ct, 8, stride=8), :]
-            s_s[b, lanes] = recv[d, t, pl.ds(64 + ct, NS - 8, stride=8), :]
-        s_s[a, NX - 128:] = block_turn(recv[d, t, 104:112, :])
+            s_s[b, lanes] = recv[d, t, pl.ds(72 + ct, NS - 8, stride=8), :]
+        s_s[a, NX - 128:] = block_turn(recv[d, t, 64:72, :])
         s_s[b, NX - 128:] = block_turn(recv[d, t, 112:120, :])[:NS - 8]
     q_s[...] = mul(pick_s[...], split(s_s[...], 2))
     c_s[...] = mul(sum_s[...], split(q_s[...] * th_s[...], 2))
@@ -239,7 +247,7 @@
 
 
 def kernel(lat_axis, cnt_ref, x_hbm, clon_hbm, clat_hbm, thick_ref, eta_ref, done, late, pick_o, th_o, idx_o, dt_o, rt_o,
-           xs, rows, clon, clat, cnorth, wlat, wedge, wlon, edge_s, sten, taps, faces, held, send, recv,
+           xs, rows, clon, clat, cnorth, wlat, wedge, wlon, edge_s, sten, taps, faces, part, held, send, recv,
            pick_s, sum_s, su_s, th_s, idx_s, dt_s, rt_s, fr_s, s_s, q_s, c_s, f_s, stage,
            x_sem, c_sem, esem, hsend, hrecv, held_sem, rest_sem, ssem, rsem, lsem, psem, osem):
     lat, lev = lax.axis_index("lat"), lax.axis_index("lev")
@@ -405,12 +413,18 @@
         return pltpu.make_async_remote_copy(send.at[t, e], late.at[lev] if last else recv.at[lev, t], ssem.at[t, k], rsem.at[t, lev],
                                             device_id=(lat, e), device_id_type=MESH)
 
+    def across_part(t, k, lo, hi):
+        e = peer(k)
+        return pltpu.make_async_remote_copy(send.at[t, e, lo:hi], recv.at[lev, t, lo:hi], ssem.at[t, k], rsem.at[t, lev],
+                                            device_id=(lat, e), device_id_type=MESH)
+
     def own(t, last=False):
         return pltpu.make_async_copy(send.at[t, lev], late.at[lev] if last else recv.at[lev, t], lsem.at[t])
 
     def forward(t, _):
+        pltpu.make_async_copy(x_hbm.at[t], xs.at[t], x_sem.at[t]).wait()
+        longitude(t, xs, wlon, sten, taps, faces, part)
         relay(t + 1)
-        pltpu.make_async_copy(x_hbm.at[t], xs.at[t], x_sem.at[t]).wait()
 
         bent = lax.rem(t, LINES) > 0
         from_above, from_below = bent & (lat == below), bent & (lat == above)
@@ -436,9 +450,22 @@
                 up_rest(t, j).wait_recv()
 
         edges(t, rows, xs, wedge, edge_s)
-        horizontal(t, xs, rows, edge_s, wlat, wlon, sten, taps, faces, send)
-
-        @pl.when(t < NT - 1)
+        latitude(t, range(8), xs, rows, edge_s, wlat, part, send)
+
+        @pl.when(t == 0)
+        def _():
+            for k in ORDER:
+                across_part(t, k, 0, HEAD).start()
+
+        latitude(t, range(8, NS), xs, rows, edge_s, wlat, part, send)
+
+        @pl.when(t == 0)
+        def _():
+            for k in ORDER:
+                across_part(t, k, HEAD, ROWS).start()
+            own(t).start()
+
+        @pl.when((t > 0) & (t < NT - 1))
         def _():
             for k in ORDER:
                 across(t, k).start()
@@ -581,6 +608,7 @@
             pltpu.VMEM((512, 512), jnp.bfloat16),
             pltpu.VMEM((9 * 112, 512), jnp.bfloat16),
             pltpu.VMEM((9 * 112, 512), F32),
+            pltpu.VMEM((NS, NI, NX), F32),
             pltpu.VMEM((HELD, 3, NS, NX), F32),
             pltpu.VMEM((NT, ND, ROWS, 128), F32),
             pltpu.VMEM((ND, NT, ROWS, 128), F32),

time: 69.3 us -> 68.7 us (level)
  no operation moved by 1% of the time
where the time goes in v5:
time: 68.7 us; the launch traced here: 68.6 us
  Pallas kernels  68.6 us (100%)
    pallas_call x1, Pallas kernels, shards(): pl.pallas_call(functools.partial(kernel, lax.axis_size('lat')), name='tra...  63 us
    pallas_call x1, Pallas kernels, shards(): pl.pallas_call(finish, name='finish', out_shape=jax.ShapeDtypeStruct((NT,...  5.52 us

profile of v5, /device:TPU:1, one launch (start us, length us, event | category | flops | bytes accessed | tf_op | source)
XLA Modules:
  0.0 68.6 jit_solution(5764889128866109864)
XLA Ops:
  0.0 63.0 %transport.1 = (f32[7,8,72,144]{3,2,1,0:T(8,128)}, f32[8,120,128]{2,1,0:T(8,128)}, f32[72,208]{1,0:T(8,128)}, f32[72,1152]{1,0:T(8,128)}, s32[9,72,128]{2,1,0:T(...) custom-call(s32[8]{0:T(128)} %cnt_ref.1, f32[8,13,8,1152]{3,2,1,0:T(8,128)} %bitcast.4, f32[13,8,1152]{2,1,0:T(8,128)} %bitcast.5, ...), custom_call_target="tpu_custom_call" | custom-call | tf_op jit(solution)/shard_map/transport/pallas_call | solution.py:591
  63.0 5.5 %finish.1 = f32[8,8,72,144]{3,2,1,0:T(8,128)} custom-call(f32[7,8,72,144]{3,2,1,0:T(8,128)} %get-tuple-element.12.done, f32[8,120,128]{2,1,0:T(8,128)} %get-tuple-element.13.late, f32[72,208]{1,0:T(8,128)} %get-tuple-element.14.pick_h, f32[72,1152]{1,0:T(8,128)} %get-tuple-element.15.th_h, s32[9,72,128]{2,1,0:T(8,128)} %get-tuple-element.16.idx_h, ...), custom_call_target="tpu_custom_call" | custom-call | tf_op jit(solution)/shard_map/finish/pallas_call | solution.py:644

commit v6 on v5

--- a/solution.py
+++ b/solution.py
@@ -205,7 +205,7 @@
     return gather(p, ((16 * r - (l & 112)) & 127) + (l & 15), 1)
 
 
-def remap_tracer(lev, t, slot, recv, stage, pick_s, sum_s, th_s, idx_s, dt_s, rt_s, s_s, q_s, c_s, f_s, beside=None):
+def remap_tracer(lev, t, slot, recv, stage, pick_s, sum_s, th_s, idx_s, dt_s, rt_s, s_s, q_s, c_s, f_s, ready=None, before=None, after=None):
     for d in range(ND):
         a, b = slice(NS * d, NS * d + 8), slice(NS * d + 8, NS * d + NS)
         for ct in range(NI):
@@ -217,6 +217,8 @@
     q_s[...] = mul(pick_s[...], split(s_s[...], 2))
     c_s[...] = mul(sum_s[...], split(q_s[...] * th_s[...], 2))
     f_s[0:8, :] = jnp.zeros((8, 128), F32)
+    if ready is not None:
+        ready()
 
     def tile(ct):
         lanes = pl.ds(ct * 128, 128) if isinstance(ct, int) else pl.ds(pl.multiple_of(ct * 128, 128), 128)
@@ -234,16 +236,19 @@
             f_s[8 + 8 * tb:16 + 8 * tb, :] = gc + dt_s[ct, at, :] * gq
         return (f_s[8:80, :] - f_s[7:79, :]) * rt_s[ct]
 
-    def main(ct, _):
-        if beside is not None:
-            beside(ct)
-        stage[slot, ct, :, 0:128] = pltpu.roll(tile(ct), lax.rem(128 - 16 * lev, 128), 1)
-        return 0
-
-    lax.fori_loop(0, NI, main, 0)
     res = tile(NI)
     for i in range(NI):
         stage[slot, i, :, 128:SPAN] = res[:, 16 * i:16 * i + 16]
+
+    def main(ct, _):
+        if before is not None:
+            before(ct)
+        stage[slot, ct, :, 0:128] = pltpu.roll(tile(ct), lax.rem(128 - 16 * lev, 128), 1)
+        if after is not None:
+            after(ct)
+        return 0
+
+    lax.fori_loop(0, NI, main, 0)
 
 
 def kernel(lat_axis, cnt_ref, x_hbm, clon_hbm, clat_hbm, thick_ref, eta_ref, done, late, pick_o, th_o, idx_o, dt_o, rt_o,
@@ -548,7 +553,7 @@
 
 
 def finish(done, late, pick_h, th_h, idx_h, dt_h, rt_h, out, recv, pick_s, sum_s, th_s, idx_s, dt_s, rt_s, s_s, q_s, c_s, f_s, stage,
-           isem, csem, osem):
+           isem, csem, osem, wsem):
     loads = [pltpu.make_async_copy(h, v, isem.at[i]) for i, (h, v) in enumerate(
         ((late, recv.at[:, 0]), (pick_h, pick_s), (th_h, th_s), (idx_h, idx_s), (dt_h, dt_s), (rt_h, rt_s)))]
 
@@ -563,18 +568,27 @@
         def _():
             fetch(t).wait()
             write(t).start()
+
+    def write_row(i):
+        return pltpu.make_async_copy(stage.at[NT - 1, i], out.at[NT - 1, i], wsem.at[i])
+
+    def ready():
+        for c in loads[3:]:
+            c.wait()
 
     for c in loads:
         c.start()
     for t in range(NT - 1):
         fetch(t).start()
     sum_s[...] = below_sum()
-    for c in loads:
+    for c in loads[:3]:
         c.wait()
-    remap_tracer(lax.axis_index("lev"), 0, NT - 1, recv, stage, pick_s, sum_s, th_s, idx_s, dt_s, rt_s, s_s, q_s, c_s, f_s, lay_down)
-    write(NT - 1).start()
-    for t in range(NT):
+    remap_tracer(lax.axis_index("lev"), 0, NT - 1, recv, stage, pick_s, sum_s, th_s, idx_s, dt_s, rt_s, s_s, q_s, c_s, f_s,
+                 ready, lay_down, lambda i: write_row(i).start())
+    for t in range(NT - 1):
         write(t).wait()
+    for i in range(NI):
+        write_row(i).wait()
 
 
 def shards(tracers, courant_lon, courant_lat, level_counts, thick_source, eta_weights):
@@ -650,7 +664,7 @@
         scratch_shapes=[
             pltpu.VMEM((ND, 1, ROWS, 128), F32), pick, sums, thick, places, tile9, tile9,
             pltpu.VMEM((SLOTS, NX), F32), pltpu.VMEM((NK, NX), F32), pltpu.VMEM((NK + 8, NX), F32), pltpu.VMEM((NK + 8, 128), F32),
-            pltpu.VMEM((NT, NI, NK, SPAN), F32), dma((6,)), dma((NT - 1,)), dma((NT,)),
+            pltpu.VMEM((NT, NI, NK, SPAN), F32), dma((6,)), dma((NT - 1,)), dma((NT - 1,)), dma((NI,)),
         ],
         compiler_params=pltpu.CompilerParams(vmem_limit_bytes=VMEM2 << 20),
     )(*parts)

time: 68.7 us -> 68.3 us (level)
  no operation moved by 1% of the time
where the time goes in v6:
time: 68.3 us; the launch traced here: 68.2 us
  Pallas kernels  68.2 us (100%)
    pallas_call x1, Pallas kernels, shards(): pl.pallas_call(functools.partial(kernel, lax.axis_size('lat')), name='tra...  63 us
    pallas_call x1, Pallas kernels, shards(): pl.pallas_call(finish, name='finish', out_shape=jax.ShapeDtypeStruct((NT,...  5.13 us

profile of v6, /device:TPU:1, one launch (start us, length us, event | category | flops | bytes accessed | tf_op | source)
XLA Modules:
  0.0 68.2 jit_solution(845643556985077204)
XLA Ops:
  0.0 63.0 %transport.1 = (f32[7,8,72,144]{3,2,1,0:T(8,128)}, f32[8,120,128]{2,1,0:T(8,128)}, f32[72,208]{1,0:T(8,128)}, f32[72,1152]{1,0:T(8,128)}, s32[9,72,128]{2,1,0:T(...) custom-call(s32[8]{0:T(128)} %cnt_ref.1, f32[8,13,8,1152]{3,2,1,0:T(8,128)} %bitcast.4, f32[13,8,1152]{2,1,0:T(8,128)} %bitcast.5, ...), custom_call_target="tpu_custom_call" | custom-call | tf_op jit(solution)/shard_map/transport/pallas_call | solution.py:605
  63.0 5.1 %finish.1 = f32[8,8,72,144]{3,2,1,0:T(8,128)} custom-call(f32[7,8,72,144]{3,2,1,0:T(8,128)} %get-tuple-element.12.done, f32[8,120,128]{2,1,0:T(8,128)} %get-tuple-element.13.late, f32[72,208]{1,0:T(8,128)} %get-tuple-element.14.pick_h, f32[72,1152]{1,0:T(8,128)} %get-tuple-element.15.th_h, s32[9,72,128]{2,1,0:T(8,128)} %get-tuple-element.16.idx_h, ...), custom_call_target="tpu_custom_call" | custom-call | tf_op jit(solution)/shard_map/finish/pallas_call | solution.py:658

commit v7 on v6

--- a/solution.py
+++ b/solution.py
@@ -16,7 +16,7 @@
 LINES = 3
 HELD = -(-NT // LINES)
 VMEM1, VMEM2 = 57, 57
-ORDER = (1, 7, 2, 6, 3, 5, 4)
+MOVES = ((2, 1), (1, 1), (3, 1), (0, 1), (2, 0), (1, 0), (3, 0))
 
 
 def gather(v, idx, axis):
@@ -265,7 +265,8 @@
     loads[0].start()
 
     def peer(k):
-        return lax.rem(lev + k, ND)
+        y, z = MOVES[k - 1]
+        return lax.rem(lev // 2 + y, 4) * 2 + lax.rem(lev + z, 2)
 
     bar = pltpu.get_barrier_semaphore()
     for k in range(1, ND):
@@ -459,26 +460,26 @@
 
         @pl.when(t == 0)
         def _():
-            for k in ORDER:
+            for k in range(1, ND):
                 across_part(t, k, 0, HEAD).start()
 
         latitude(t, range(8, NS), xs, rows, edge_s, wlat, part, send)
 
         @pl.when(t == 0)
         def _():
-            for k in ORDER:
+            for k in range(1, ND):
                 across_part(t, k, HEAD, ROWS).start()
             own(t).start()
 
         @pl.when((t > 0) & (t < NT - 1))
         def _():
-            for k in ORDER:
+            for k in range(1, ND):
                 across(t, k).start()
             own(t).start()
 
         @pl.when(t == NT - 1)
         def _():
-            for k in ORDER:
+            for k in range(1, ND):
                 across(t, k, True).start()
             own(t, True).start()
         return 0

time: 68.3 us -> 69.6 us (1.019)
  Pallas kernels: 68.2 us -> 69.5 us
    pallas_call x1, Pallas kernels: 63 us -> 64.4 us  [shards(): pl.pallas_call(functools.partial(kernel, lax.axis_size('lat')), name='tra...]
where the time goes in v7:
time: 69.6 us; the launch traced here: 69.5 us
  Pallas kernels  69.5 us (100%)
    pallas_call x1, Pallas kernels, shards(): pl.pallas_call(functools.partial(kernel, lax.axis_size('lat')), name='tra...  64.4 us
    pallas_call x1, Pallas kernels, shards(): pl.pallas_call(finish, name='finish', out_shape=jax.ShapeDtypeStruct((NT,...  5.13 us

profile of v7, /device:TPU:1, one launch (start us, length us, event | category | flops | bytes accessed | tf_op | source)
XLA Modules:
  0.0 69.5 jit_solution(4587459635054104388)
XLA Ops:
  0.0 64.4 %transport.1 = (f32[7,8,72,144]{3,2,1,0:T(8,128)}, f32[8,120,128]{2,1,0:T(8,128)}, f32[72,208]{1,0:T(8,128)}, f32[72,1152]{1,0:T(8,128)}, s32[9,72,128]{2,1,0:T(...) custom-call(s32[8]{0:T(128)} %cnt_ref.1, f32[8,13,8,1152]{3,2,1,0:T(8,128)} %bitcast.4, f32[13,8,1152]{2,1,0:T(8,128)} %bitcast.5, ...), custom_call_target="tpu_custom_call" | custom-call | tf_op jit(solution)/shard_map/transport/pallas_call | solution.py:606
  64.4 5.1 %finish.1 = f32[8,8,72,144]{3,2,1,0:T(8,128)} custom-call(f32[7,8,72,144]{3,2,1,0:T(8,128)} %get-tuple-element.12.done, f32[8,120,128]{2,1,0:T(8,128)} %get-tuple-element.13.late, f32[72,208]{1,0:T(8,128)} %get-tuple-element.14.pick_h, f32[72,1152]{1,0:T(8,128)} %get-tuple-element.15.th_h, s32[9,72,128]{2,1,0:T(8,128)} %get-tuple-element.16.idx_h, ...), custom_call_target="tpu_custom_call" | custom-call | tf_op jit(solution)/shard_map/finish/pallas_call | solution.py:659
